TPU v7x, 512 devices: a whole 4x4x16 slice. The times are simulated.
512 devices in a mesh: member: 32 (over x, z_hi, y), mp: 16 (over z_lo, core).
Axes of the slice: x: 4, y: 4, z: 16 (z_hi: 2, z_lo: 8; z = z_hi * 8 + z_lo), core: 2. Of those that a mesh axis runs over, the one named last changes fastest.
Arguments:
- grid_fields: bfloat16 [32, 27648, 128], P('member', 'mp'), may hold values from -6 to 6
- edge_grid: int32 [2048, 32], P('mp'), may hold values from 0 to 27647, as said below
- edge_count: int32 [2048], P('mp'), may hold values from 16 to 32
- edge_weight: float32 [2048, 32], P('mp'), may hold values from 0.1 to 1
- enc_weight: bfloat16 [128, 1024], replicated, may hold values from -0.0625 to 0.0625
- qkv_weight: bfloat16 [3, 1024, 1024], P(None, 'mp')
- out_weight: bfloat16 [1024, 1024], P('mp'), may hold values from -0.75 to 0.75
- cotangent: bfloat16 [32, 2048, 1024], P('member', 'mp'), may hold values from -0.29882812 to 0.29882812
Outputs:
- layer_out: bfloat16 [32, 2048, 1024], P('member', 'mp')
- grad_qkv: float32 [3, 1024, 1024], P(None, 'mp')
- grad_out: float32 [1024, 1024], P('mp')
Inputs may be any that keep to these rules, and one draw needn't show every extreme that they name: edge_grid[n, k] lies within 864 rows of the centre of node n's share of the grid, so its block of 1728 rows is n // 128 - 1, n // 128 or n // 128 + 1; slot 0 of the first node of each block of 128 nodes reaches the block before and slot 0 of its last node the block after, where those exist; slots at or after edge_count hold valid rows too.
All inputs are finite; a program needn't handle non-finite values.
Results may differ from a plain program's by a relative error of at most 0.03.
Values may be sent and summed in bfloat16 or wider, within the bound.
A program may use at most 128 MiB of HBM per device.

v0:
```python
import jax
import jax.numpy as jnp
from jax import lax
from jax.sharding import PartitionSpec as P

D = 1024
HEADS = 16
WINDOW = 512
GRID_DEV = 1728


def padded(cells, sides, width):
    for axis, dim in sides:
        count = lax.axis_size(axis)
        ends = count - 1
        head = lax.slice_in_dim(cells, 0, width, axis=dim)
        tail = lax.slice_in_dim(cells, cells.shape[dim] - width, cells.shape[dim], axis=dim)
        cells = jnp.concatenate(
            [
                lax.ppermute(tail, axis, [(i, (i + 1) % count) for i in range(ends)]),
                cells,
                lax.ppermute(head, axis, [((i + 1) % count, i) for i in range(ends)]),
            ],
            axis=dim,
        )
    return cells


def layer_norm(hidden):
    centred = hidden - jnp.mean(hidden, axis=-1, keepdims=True)
    spread = jnp.mean(centred * centred, axis=-1, keepdims=True)
    return centred * lax.rsqrt(spread + 1e-05)


def window_attention(queries, key_rows, value_rows):
    length = queries.shape[0]
    head_count = queries.shape[1]
    head_width = queries.shape[2]
    block_rows = min(512, length)
    half_span = WINDOW // 2
    key_span = block_rows + 2 * half_span
    score_scale = 1.0 / head_width**0.5
    padding = jnp.zeros((half_span, head_count, head_width), queries.dtype)
    key_padded = jnp.concatenate([padding, key_rows, padding], axis=0)
    value_padded = jnp.concatenate([padding, value_rows, padding], axis=0)

    def one_block(block_start):
        query_block = lax.dynamic_slice_in_dim(queries, block_start, block_rows, 0)
        key_block = lax.dynamic_slice_in_dim(key_padded, block_start, key_span, 0)
        value_block = lax.dynamic_slice_in_dim(value_padded, block_start, key_span, 0)
        scores = (
            jnp.einsum("ihe,jhe->hij", query_block, key_block, preferred_element_type=jnp.float32)
            * score_scale
        )
        row_pos = block_start + jnp.arange(block_rows, dtype=jnp.int32)
        col_pos = block_start - half_span + jnp.arange(key_span, dtype=jnp.int32)
        inside = (
            (col_pos[None, :] >= 0)
            & (col_pos[None, :] < length)
            & (jnp.abs(row_pos[:, None] - col_pos[None, :]) <= half_span)
        )
        scores = jnp.where(inside[None], scores, -1e30)
        row_max = jnp.max(scores, axis=2, keepdims=True)
        weights = jnp.where(inside[None], jnp.exp(scores - row_max), 0.0)
        row_total = jnp.sum(weights, axis=2, keepdims=True)
        probability = (weights / row_total).astype(jnp.bfloat16)
        return jnp.einsum(
            "hij,jhe->ihe", probability, value_block, preferred_element_type=jnp.float32
        )

    block_starts = jnp.arange(length // block_rows, dtype=jnp.int32) * block_rows
    stacked = lax.map(one_block, block_starts)
    return stacked.reshape(length, head_count, head_width)


def on_device(
    grid_fields, edge_grid, edge_count, edge_weight, enc_weight, qkv_weight, out_weight, cotangent
):
    grid_block = grid_fields[0]
    position = lax.axis_index("mp")
    slot_ids = jnp.arange(edge_grid.shape[1], dtype=jnp.int32)
    coeffs = jnp.where(slot_ids[None, :] < edge_count[:, None], edge_weight, 0.0)
    extended = padded(grid_block, (("mp", 0),), GRID_DEV)
    local_index = edge_grid - (position - 1) * GRID_DEV
    picked = jnp.take(extended, local_index, axis=0).astype(jnp.float32)
    node_sum = jnp.sum(coeffs[:, :, None] * picked, axis=1)
    node_in = node_sum.astype(jnp.bfloat16)
    hidden = jnp.dot(node_in, enc_weight, preferred_element_type=jnp.float32)
    normed = layer_norm(hidden).astype(jnp.bfloat16)
    gathered = lax.all_gather(normed, "mp", axis=0, tiled=True)
    total_rows = gathered.shape[0]
    head_width = D // HEADS
    local_heads = qkv_weight.shape[1] // head_width
    projected = jnp.einsum(
        "nd,cfd->cnf", gathered, qkv_weight, preferred_element_type=jnp.float32
    ).astype(jnp.bfloat16)
    shaped = projected.reshape(3, total_rows, local_heads, head_width)
    attended_f, back_fn = jax.vjp(window_attention, shaped[0], shaped[1], shaped[2])
    attended = attended_f.astype(jnp.bfloat16).reshape(total_rows, local_heads * head_width)
    node_attended = lax.all_to_all(attended, "mp", split_axis=0, concat_axis=1, tiled=True)
    full_out = lax.all_gather(out_weight, "mp", axis=0, tiled=True)
    layer_out = (
        hidden + jnp.dot(node_attended, full_out, preferred_element_type=jnp.float32)
    ).astype(jnp.bfloat16)
    cot_rows = cotangent[0]
    contract_cols = (((1,), (1,)), ((), ()))
    contract_rows = (((0,), (0,)), ((), ()))
    cot_all = lax.all_gather(cot_rows, "mp", axis=0, tiled=True)
    d_attended = lax.dot_general(
        cot_all, out_weight, contract_cols, preferred_element_type=jnp.float32
    ).astype(jnp.bfloat16)
    grad_out = lax.dot_general(attended, cot_all, contract_rows, preferred_element_type=jnp.float32)
    cot_grads = back_fn(d_attended.reshape(total_rows, local_heads, head_width).astype(jnp.float32))
    d_projected = jnp.stack(cot_grads).reshape(3, total_rows, local_heads * head_width)
    grad_qkv = jnp.einsum("cnf,nd->cfd", d_projected, gathered, preferred_element_type=jnp.float32)
    grad_qkv, grad_out = (
        lax.psum(grad_qkv.astype(jnp.bfloat16), "member").astype(jnp.float32),
        lax.psum(grad_out.astype(jnp.bfloat16), "member").astype(jnp.float32),
    )
    return (layer_out[None], grad_qkv, grad_out)


def solution(mesh):
    placed = (
        P("member", "mp", None),
        P("mp", None),
        P("mp"),
        P("mp", None),
        P(),
        P(None, "mp", None),
        P("mp", None),
        P("member", "mp", None),
    )
    return jax.shard_map(
        on_device,
        mesh=mesh,
        in_specs=placed,
        out_specs=(P("member", "mp", None), P(None, "mp", None), P("mp", None)),
        check_vma=False,
    )
```

profile of v0, /device:TPU:6, one launch (start us, length us, event | category | flops | bytes accessed | tf_op | source)
XLA Modules:
  0.0 1106.6 jit_solution(17828965656435089373)
XLA Ops:
  12.9 2.4 collective-permute-done.1
  16.4 12.1 %gather_fusion = bf16[4096,128]{1,0:T(8,128)(2,1)S(1)} fusion(bf16[5184,128]{1,0:T(8,128)(2,1)S(1)} %pad_maximum_fusion, s32[4096]{0:T(1024)S(1)} %broadcast_clamp_fusion), kind=kCustom, calls=%fused_computation | custom fusion | bytes 2113536 | tf_op jit(solution)/shard_map/jit(_take)/gather | solution.py:85
  32.5 88.8 %all-gather.9.cloned.1.call-done = bf16[1,2048,1024]{2,1,0:T(8,128)(2,1)} async-done(((bf16[1,128,1024]{2,1,0:T(8,128)(2,1)}), bf16[1,2048,1024]{2,1,0:T(8,128)(2,1)}) %all-gather.9.cloned.1.call-update) | async-done | bytes 4194320 | tf_op jit(solution)/shard_map/all_gather | solution.py:108
  121.3 3.6 fusion.64
  126.2 102.1 %all-gather.5.cloned.1.call-done = bf16[2048,1024]{1,0:T(8,128)(2,1)} async-done(((bf16[128,1024]{1,0:T(8,128)(2,1)}), bf16[2048,1024]{1,0:T(8,128)(2,1)}) %all-gather.5.cloned.1.call-update) | async-done | bytes 4194320 | tf_op jit(solution)/shard_map/all_gather | solution.py:90
  228.3 3.7 fusion.58
  232.2 80.8 %while.63 = (s32[]{:T(128)}, bf16[4,512,1,64]{1,3,2,0:T(8,128)(2,1)}, s32[4]{0:T(128)}, s32[4]{0:T(128)}, bf16[4,1024,1,64]{1,3,2,0:T(8,128)(2,1)}, /*index=5*/b...) while((s32[]{:T(128)}, ...), condition=%wide.region_7.8_spmd.clone, body=%wide.region_3.0_spmd.clone.sunk | while | flops 153097216 | bytes 22682008 | solution.py:72
  240.4 3.4 bitcast_dynamic-update-slice_fusion.13
  260.5 3.5 bitcast_dynamic-update-slice_fusion.13
  280.7 3.4 bitcast_dynamic-update-slice_fusion.13
  300.8 3.5 bitcast_dynamic-update-slice_fusion.13
  315.3 96.0 %while.62 = (s32[]{:T(128)}, bf16[2048,1,64]{0,2,1:T(8,128)(2,1)}, bf16[2560,1,64]{0,2,1:T(8,128)(2,1)}, bf16[2560,1,64]{0,2,1:T(8,128)(2,1)}, s32[4]{0:T(128)},...) while((s32[]{:T(128)}, bf16[2048,1,64]{0,2,1:T(8,128)(2,1)}, ...), condition=%wide.region_11.12_spmd, body=%wide.region_8.11_spmd.sunk | while | flops 278626816 | bytes 21603072 | solution.py:72
  318.4 2.4 fusion.122
  322.7 3.0 fusion.124
  329.3 3.1 fusion.123
  342.3 2.4 fusion.122
  346.6 3.0 fusion.124
  353.2 3.1 fusion.123
  366.3 2.4 fusion.122
  370.6 3.0 fusion.124
  377.2 3.1 fusion.123
  384.8 2.4 add_any.53
  390.3 2.4 fusion.122
  394.7 3.0 fusion.124
  397.7 2.3 add_any.52
  401.3 3.1 fusion.123
  408.9 2.3 add_any.53
  413.6 3.8 fusion.72
  420.7 7.3 all-to-all-start
  428.0 549.3 %all-reduce.3.cloned.1.call-done = (bf16[3,64,1024]{2,1,0:T(8,128)(2,1)}, bf16[64,1024]{1,0:T(8,128)(2,1)}) async-done(((bf16[3,64,1024]{2,1,0:T(8,128)(2,1)}, bf16[64,1024]{1,0:T(8,128)(2,1)}), (bf16[3,64,1024]{2,1,0:T(8,128)(2,1)}, bf16[64,1024]{1,0:T(8,128)(2,1)})) %all-reduce.3.cloned.1.call-update) | async-done | bytes 524304 | tf_op jit(solution)/shard_map/psum | solution.py:117
  980.9 116.4 %all-gather.7.cloned.1.call-done = bf16[1024,1024]{1,0:T(8,128)(2,1)} async-done(((bf16[64,1024]{1,0:T(8,128)(2,1)}), bf16[1024,1024]{1,0:T(8,128)(2,1)}) %all-gather.7.cloned.1.call-update) | async-done | bytes 2097168 | tf_op jit(solution)/shard_map/all_gather | solution.py:101
  1097.3 2.8 fusion.71
  (185 shorter events, 128.5 us)
Async XLA Ops:
  7.2 221.2 %copy-start = (bf16[3,64,1024]{2,1,0:T(8,128)(2,1)S(1)}, bf16[3,64,1024]{2,1,0:T(8,128)(2,1)}, u32[]{:S(2)}) copy-start(bf16[3,64,1024]{2,1,0:T(8,128)(2,1)} %param.17) | copy-start | bytes 1179652
  7.2 114.1 %all-gather.9.cloned.1.call-start = ((), (), s32[]{:S(2)}) async-start(), calls=%async_computation.3 | async-start | bytes 4456448 | tf_op jit(solution)/shard_map/all_gather | solution.py:108
  7.9 220.4 %all-gather.5.cloned.1.call-start = ((), (), s32[]{:S(2)}) async-start(), calls=%async_computation.1 | async-start | bytes 4456448 | tf_op jit(solution)/shard_map/all_gather | solution.py:90
  8.0 5.0 collective-permute-start
  9.7 5.6 collective-permute-start.1
  28.6 92.7 %copy-start.2 = (bf16[64,1024]{1,0:T(8,128)(2,1)S(1)}, bf16[64,1024]{1,0:T(8,128)(2,1)}, u32[]{:S(2)}) copy-start(bf16[64,1024]{1,0:T(8,128)(2,1)} %param.18) | copy-start | bytes 393220
  32.3 945.0 %all-reduce.3.cloned.1.call-start = ((), (), s32[]{:S(2)}) async-start(), calls=%async_computation.4 | async-start | bytes 1048576 | tf_op jit(solution)/shard_map/psum | solution.py:117
  243.8 2.0 copy-start.3
  246.3 6.3 copy-start.4
  264.0 2.0 copy-start.3
  266.4 6.3 copy-start.4
  284.1 2.0 copy-start.3
  286.5 6.2 copy-start.4
  304.3 2.0 copy-start.3
  306.8 6.2 copy-start.4
  413.5 3.9 copy-start.1
  413.5 3.9 copy-start.5
  419.2 678.1 %all-gather.7.cloned.1.call-start = ((), (), s32[]{:S(2)}) async-start(), calls=%async_computation.2 | async-start | bytes 2228224 | tf_op jit(solution)/shard_map/all_gather | solution.py:101
  420.7 676.6 %all-to-all-start = ((bf16[16,128,64]{1,2,0:T(8,128)(2,1)}), bf16[16,128,64]{1,2,0:T(8,128)(2,1)S(1)}, u32[]{:S(2)}, u32[]{:S(2)}) async-start(bf16[16,128,64]{1,2,0:T(8,128)(2,1)} %copy.28), calls=%async_computation | async-start | bytes 524288 | tf_op jit(solution)/shard_map/all_to_all | solution.py:100
Sparse Core Ops, SparseCore 0:
  10.1 111.1 all-gather.8
  123.4 104.9 all-gather.4
  419.3 557.9 all-reduce.2
  979.4 117.7 all-gather.6
where the time goes:
time: 1110 us
  waiting for transfers between devices  860 us (77%)
  local copies, waits for them, and re-layouts  85.3 us (8%)
  matrix products  65 us (6%)
  other arithmetic  54.8 us (5%)
  loops' own time  16.7 us (2%)
  between operations  14 us (1%)
    psum x1, waiting for transfers between devices, on_device(): lax.psum(grad_qkv.astype(jnp.bfloat16), 'member').astype(jnp.float32)  549 us
    all_gather x1, waiting for transfers between devices, on_device(): full_out = lax.all_gather(out_weight, 'mp', axis=0, tiled=True)  116 us
    all_gather x1, waiting for transfers between devices, on_device(): gathered = lax.all_gather(normed, 'mp', axis=0, tiled=True)  102 us
    all_gather x1, waiting for transfers between devices, on_device(): cot_all = lax.all_gather(cot_rows, 'mp', axis=0, tiled=True)  88.8 us
    dot_general x12, matrix products, one_block(): jnp.einsum('ihe,jhe->hij', query_block, key_block, preferred_element_type...  29 us
    dynamic_update_slice x16, other arithmetic, window_attention(): stacked = lax.map(one_block, block_starts)  27.7 us
  transfers between devices with their start and end apart: 7, of which 5 were waited for; matrix products, arithmetic and copies ran while one was open for 3% of the time, Pallas kernels for 0%

commit v1 on v0

v1 whole, which is shorter than its diff:
```python
import functools
import math

import jax
import jax.numpy as jnp
from jax import lax
from jax.experimental import pallas as pl
from jax.experimental.pallas import tpu as pltpu
from jax.sharding import PartitionSpec as P

MESH = pl.DeviceIdType.MESH
BF16, F32 = jnp.bfloat16, jnp.float32
LOG2E = math.log2(math.e)

GRID_DEV = 1728
EXT = 41 * 128
BAND = 17 * 128
KEYS = 768
NT = (((1,), (1,)), ((), ()))
SHARD_AT = {0: 0, 4: 0, 7: 1, 3: 1, 1: 2, 5: 2, 2: 3, 6: 3}


def dot(a, b):
    return jnp.dot(a, b, preferred_element_type=F32)


def dot_nt(a, b):
    return lax.dot_general(a, b, NT, preferred_element_type=F32)


def attention_scratch():
    return dict(
        keys=pltpu.VMEM((1024, 256), BF16),
        keys_t=pltpu.VMEM((256, 1024), BF16),
        values=pltpu.VMEM((1024, 256), BF16),
        values_t=pltpu.VMEM((256, 1024), BF16),
        query=pltpu.VMEM((512, 256), BF16),
        query_tz=pltpu.VMEM((4, 128, 512), BF16),
        d_att_t=pltpu.VMEM((256, 512), BF16),
        bias=pltpu.VMEM((2, KEYS, 256), F32),
        weights=pltpu.VMEM((8, KEYS, 256), BF16),
        row_d=pltpu.VMEM((8, 1, 256), F32),
        d_att_z=pltpu.VMEM((8, 128, 256), BF16),
        att_t=pltpu.VMEM((256, 512), F32),
        d_query_t=pltpu.VMEM((256, 512), BF16),
        d_keys=pltpu.VMEM((1024, 256), F32),
        d_values=pltpu.VMEM((1024, 256), F32),
        left=pltpu.VMEM((256, 1024), BF16),
    )


def weight_grad(grads, c, left, right):
    def tile(t, carry):
        cols = pl.ds(pl.multiple_of(t * 256, 256), 256)
        product = dot(left(), right(cols)).astype(BF16)
        for j in range(4):
            grads[c, j, :, cols] = product[j * 64 : (j + 1) * 64]
        return carry

    lax.fori_loop(0, 4, tile, 0)


def attention(grp, normed, w, cot, grads, part, s, after_forward):
    key_pos = lax.broadcasted_iota(jnp.int32, (KEYS, 256), 0)
    query_pos = lax.broadcasted_iota(jnp.int32, (KEYS, 256), 1)
    for qb in range(2):
        node = key_pos + (grp * 512 - 256 + qb * 256)
        inside = (key_pos >= query_pos) & (key_pos <= query_pos + 512) & (node >= 0) & (node < 2048)
        s.bias[qb] = jnp.where(inside, 0.0, -1e30)
    s.d_keys[...] = jnp.zeros_like(s.d_keys)
    s.d_values[...] = jnp.zeros_like(s.d_values)

    wq = w[:, 0].reshape(256, 1024)
    wk = w[:, 1].reshape(256, 1024)
    wv = w[:, 2].reshape(256, 1024)
    wo = w[:, 3].reshape(256, 1024)

    def project(t, carry):
        rows = pl.ds(pl.multiple_of(t * 256, 256), 256)
        block = normed[rows, :]
        s.keys[rows, :] = dot_nt(block, wk).astype(BF16)
        s.values[rows, :] = dot_nt(block, wv).astype(BF16)
        s.keys_t[:, rows] = dot_nt(wk, block).astype(BF16)
        s.values_t[:, rows] = dot_nt(wv, block).astype(BF16)
        return carry

    lax.fori_loop(0, 4, project, 0)

    def project_own(t, carry):
        rows = pl.ds(pl.multiple_of(t * 256, 256), 256)
        block = normed[pl.ds(pl.multiple_of(t * 256 + 256, 256), 256), :]
        s.query[rows, :] = (dot_nt(block, wq) * (LOG2E / 8)).astype(BF16)
        query_t = dot_nt(wq, block) * (LOG2E / 8)
        upper = lax.broadcasted_iota(jnp.int32, (128, 256), 0) < 64
        for h in range(4):
            pair = query_t[h // 2 * 128 : h // 2 * 128 + 128]
            keep = upper if h % 2 == 0 else ~upper
            s.query_tz[h, :, rows] = jnp.where(keep, pair, 0.0).astype(BF16)
        cot_rows = cot[pl.ds(t * 2, 2)].reshape(256, 1024)
        s.d_att_t[:, rows] = dot_nt(wo, cot_rows).astype(BF16)
        return carry

    lax.fori_loop(0, 2, project_own, 0)

    def place(i):
        pair, qb = lax.div(i, 2), lax.rem(i, 2)
        key_rows = pl.ds(pl.multiple_of(qb * 256, 256), KEYS)
        lanes = pl.ds(pl.multiple_of(pair * 128, 128), 128)
        cols = pl.ds(pl.multiple_of(qb * 256, 256), 256)
        return pair, qb, key_rows, lanes, cols

    def head_rows(pair, hh):
        return pl.ds(pl.multiple_of(pair * 128 + hh * 64, 64), 64)

    def forward(i, carry):
        pair, qb, key_rows, lanes, cols = place(i)
        key_block = s.keys[key_rows, lanes]
        all_weights, scaled = [], []
        for hh in range(2):
            scores = dot(key_block, s.query_tz[pair * 2 + hh, :, cols]) + s.bias[qb]
            weight = jnp.exp2(scores - jnp.max(scores, axis=0, keepdims=True))
            inverse = 1.0 / jnp.sum(weight, axis=0, keepdims=True)
            weight = weight.astype(BF16)
            s.weights[i * 2 + hh] = weight
            all_weights.append(weight)
            rows = head_rows(pair, hh)
            out = dot(s.values_t[rows, key_rows], weight) * inverse
            d_out = s.d_att_t[rows, cols].astype(F32)
            s.row_d[i * 2 + hh] = jnp.sum(d_out * out, axis=0, keepdims=True) * inverse
            s.att_t[rows, cols] = out
            scaled.append(d_out * inverse)
        both = jnp.concatenate(scaled, axis=0)
        upper = lax.broadcasted_iota(jnp.int32, (128, 256), 0) < 64
        s.d_att_z[i * 2] = jnp.where(upper, both, 0.0).astype(BF16)
        s.d_att_z[i * 2 + 1] = jnp.where(upper, 0.0, both).astype(BF16)
        rows_form = both.T
        low = lax.broadcasted_iota(jnp.int32, (256, 128), 1) < 64
        s.d_values[key_rows, lanes] += dot(
            all_weights[0], jnp.where(low, rows_form, 0.0).astype(BF16)
        ) + dot(all_weights[1], jnp.where(low, 0.0, rows_form).astype(BF16))
        return carry

    lax.fori_loop(0, 4, forward, 0)

    def project_out(t, carry):
        rows = pl.ds(pl.multiple_of(t * 128, 128), 128)
        attended = s.att_t[:, rows].T.astype(BF16)
        part[t] = dot(attended, wo).astype(BF16)
        return carry

    lax.fori_loop(0, 4, project_out, 0)
    s.left[:, 0:512] = s.att_t[...].astype(BF16)
    weight_grad(
        grads, 3, lambda: s.left[:, 0:512], lambda cols: cot[:, :, cols].reshape(512, 256)
    )
    s.left[...] = s.d_values[...].T.astype(BF16)
    weight_grad(grads, 2, lambda: s.left[...], lambda cols: normed[:, cols])
    after_forward()

    def backward(i, carry):
        pair, qb, key_rows, lanes, cols = place(i)
        value_block = s.values[key_rows, lanes]
        low = lax.broadcasted_iota(jnp.int32, (256, 128), 1) < 64
        query = s.query[cols, lanes]
        d_keys = jnp.zeros((KEYS, 128), F32)
        for hh in range(2):
            d_weight = dot(value_block, s.d_att_z[i * 2 + hh])
            d_scores = (s.weights[i * 2 + hh].astype(F32) * (d_weight - s.row_d[i * 2 + hh])).astype(BF16)
            rows = head_rows(pair, hh)
            s.d_query_t[rows, cols] = (dot(s.keys_t[rows, key_rows], d_scores) * 0.125).astype(BF16)
            d_keys += dot(d_scores, jnp.where(low if hh == 0 else ~low, query, jnp.zeros_like(query)))
        s.d_keys[key_rows, lanes] += d_keys * (1.0 / LOG2E)
        return carry

    lax.fori_loop(0, 4, backward, 0)
    weight_grad(grads, 0, lambda: s.d_query_t[...], lambda cols: normed[256:768, cols])
    s.left[...] = s.d_keys[...].T.astype(BF16)
    weight_grad(grads, 1, lambda: s.left[...], lambda cols: normed[:, cols])


class Names:
    def __init__(self, names, refs):
        self.__dict__.update(zip(names, refs, strict=True))


def exchange_scratch():
    return dict(
        ext=pltpu.VMEM((EXT, 128), BF16),
        place=pltpu.VMEM((128, EXT), BF16),
        coef=pltpu.VMEM((128, 32), F32),
        nodes=pltpu.VMEM((8, 128, 128), BF16),
        normed=pltpu.VMEM((1024, 1024), BF16),
        w=pltpu.VMEM((4, 4, 64, 1024), BF16),
        cot=pltpu.VMEM((4, 128, 1024), BF16),
        grads=pltpu.VMEM((4, 4, 64, 1024), BF16),
        part=pltpu.VMEM((4, 128, 1024), BF16),
        part_in=pltpu.VMEM((3, 128, 1024), BF16),
        in_a1=pltpu.VMEM((4, 3, 4, 16, 512), BF16),
        in_b1=pltpu.VMEM((4, 3, 4, 16, 512), BF16),
        sum_a1=pltpu.VMEM((4, 4, 16, 512), BF16),
        sum_b1=pltpu.VMEM((4, 4, 16, 512), BF16),
        in_a2=pltpu.VMEM((4, 3, 4, 16, 128), BF16),
        in_b2=pltpu.VMEM((4, 3, 4, 16, 128), BF16),
        plane=pltpu.VMEM((4, 4, 2, 16, 128), BF16),
        in_z=pltpu.VMEM((7, 2, 2, 16, 128), BF16),
        total=pltpu.VMEM((4, 2, 16, 128), BF16),
        gathered=pltpu.VMEM((4, 64, 1024), BF16),
    )


EXCHANGE = exchange_scratch()
ATTENTION = attention_scratch()
SEMS = 128


def step_kernel(*refs):
    inputs = Names(("grid", "edge", "count", "edge_w", "enc", "wqkv", "wo", "cot"), refs[:8])
    layer_out, grad_qkv, grad_out = refs[8:11]
    b = Names(tuple(EXCHANGE), refs[11 : 11 + len(EXCHANGE)])
    s = Names(tuple(ATTENTION), refs[11 + len(EXCHANGE) : 11 + len(EXCHANGE) + len(ATTENTION)])
    send_sem, recv_sem, local_sem = refs[11 + len(EXCHANGE) + len(ATTENTION) :]

    member, mp = lax.axis_index("member"), lax.axis_index("mp")
    x, hi, y = lax.div(member, 8), lax.rem(lax.div(member, 4), 2), lax.rem(member, 4)
    g = hi * 16 + mp
    r, grp = lax.rem(mp, 4), lax.div(mp, 4)

    def at_col(place):
        there = lax.rem(place + 32, 32)
        return (x * 8 + lax.div(there, 16) * 4 + y, lax.rem(there, 16))

    def at_x(d):
        return (lax.rem(x + d, 4) * 8 + hi * 4 + y, mp)

    def at_y(d):
        return (x * 8 + hi * 4 + lax.rem(y + d, 4), mp)

    def mate(d):
        return at_col(g - r + lax.rem(r + d, 4))

    started, used = [], [0]

    def take(n=1):
        used[0] += n
        return used[0] - n

    def push(src, dst, recv, device):
        copy = pltpu.make_async_remote_copy(
            src_ref=src,
            dst_ref=dst,
            send_sem=send_sem.at[len(started)],
            recv_sem=recv_sem.at[recv],
            device_id=device,
            device_id_type=MESH,
        )
        copy.start()
        started.append(copy)

    def arrived(dst, recv):
        pltpu.make_async_copy(dst, dst, recv_sem.at[recv]).wait()

    def tile16(k):
        return pl.ds(pl.multiple_of(k * 16, 16), 16)

    def tile128(k):
        return pl.ds(pl.multiple_of(k * 128, 128), 128)

    LOW, HIGH = pl.ds(0, 512), pl.ds(512, 512)

    barrier = pltpu.get_barrier_semaphore()
    sources = [at_col(g + 4 * d) for d in range(1, 8)]
    sources += [at_x(d) for d in range(1, 4)] + [at_y(d) for d in range(1, 4)]
    sources += [mate(d) for d in range(1, 4)]
    sources += [at_col(g - r + d) for d in (-2, -1, 4, 5)]
    for device in sources:
        pl.semaphore_signal(barrier, inc=1, device_id=device, device_id_type=MESH)
    own_grid = pltpu.make_async_copy(inputs.grid, b.ext.at[pl.ds(GRID_DEV, GRID_DEV)], local_sem.at[0])
    own_w = pltpu.make_async_copy(inputs.wqkv, b.w.at[0, pl.ds(0, 3)], local_sem.at[1])
    own_wo = pltpu.make_async_copy(inputs.wo, b.w.at[0, 3], local_sem.at[2])
    own_cot = pltpu.make_async_copy(inputs.cot, b.cot.at[r], local_sem.at[3])
    for copy in (own_grid, own_w, own_wo, own_cot):
        copy.start()
    pl.semaphore_wait(barrier, len(sources))

    left_rows, right_rows = pl.ds(0, GRID_DEV), pl.ds(2 * GRID_DEV, GRID_DEV)
    grid_sem = take(2)
    push(inputs.grid, b.ext.at[left_rows], grid_sem, at_col(g + 1))
    push(inputs.grid, b.ext.at[right_rows], grid_sem + 1, at_col(g - 1))

    own_w.wait()
    own_wo.wait()
    piece_a = (tile16(y), tile128(x))
    piece_b = (tile16(x), tile128(y + 4))
    ALL = slice(None)
    z_sem = take(6)
    for n, (j, off) in enumerate(((1, 4), (2, -4), (3, 8))):
        push(b.w.at[(0, ALL) + piece_a], b.w.at[(j, ALL) + piece_a], z_sem + n, at_col(g + off))
        push(b.w.at[(0, ALL) + piece_b], b.w.at[(j, ALL) + piece_b], z_sem + 3 + n, at_col(g + off))

    b.place[...] = jnp.zeros_like(b.place)
    b.ext[pl.ds(3 * GRID_DEV, EXT - 3 * GRID_DEV), :] = jnp.zeros((EXT - 3 * GRID_DEV, 128), BF16)
    counts = jnp.broadcast_to(inputs.count[...].astype(F32), (128, 128)).T[:, :32]
    slot = lax.broadcasted_iota(jnp.int32, (128, 32), 1).astype(F32)
    b.coef[...] = jnp.where(slot < counts, inputs.edge_w[...], 0.0)

    def build(k, carry):
        rows = tile16(k)
        start = pl.multiple_of(lax.div(862 + 216 * k, 128) * 128, 128)
        index = inputs.edge[rows, :] - ((mp - 1) * GRID_DEV + start)
        coef = b.coef[rows, :]
        lane = lax.broadcasted_iota(jnp.int32, (16, BAND), 1)
        total = jnp.zeros((16, BAND), F32)
        for e in range(32):
            total += jnp.where(lane == index[:, e : e + 1], coef[:, e : e + 1], 0.0)
        b.place[rows, pl.ds(start, BAND)] = total.astype(BF16)
        return carry

    lax.fori_loop(0, 8, build, 0)

    others = pl.ds(1, 3)
    w_all = b.w.at[others]
    for n in range(3):
        arrived(b.w.at[(n + 1, ALL) + piece_a], z_sem + n)
        arrived(b.w.at[(n + 1, ALL) + piece_b], z_sem + 3 + n)
    first_a, first_b = take(3), take(3)
    for d in range(1, 4):
        part_a = b.w.at[(others, ALL) + piece_a]
        part_b = b.w.at[(others, ALL) + piece_b]
        push(part_a, part_a, first_a + d - 1, at_x(d))
        push(part_b, part_b, first_b + d - 1, at_y(d))

    own_grid.wait()
    arrived(b.ext.at[left_rows], grid_sem)
    arrived(b.ext.at[right_rows], grid_sem + 1)
    node_in = dot(b.place[...], b.ext[...]).astype(BF16)
    b.nodes[pl.ds(r + 2, 1)] = node_in[None]
    mine = b.nodes.at[r + 2]
    mate_sem, next_sem = take(3), take(4)
    for d in range(1, 4):
        push(mine, mine, mate_sem + d - 1, mate(d))
    near = jnp.where(r < 2, g - r - 4, g - r + 4)
    for t in range(4):
        push(mine, b.nodes.at[lax.rem(r + 6, 8)], next_sem + r, at_col(near + t))
    own_cot.wait()
    cot_sem = take(3)
    for d in range(1, 4):
        push(b.cot.at[r], b.cot.at[r], cot_sem + d - 1, mate(d))

    second_a, second_b = take(3), take(3)
    for d in range(1, 4):
        arrived(b.w.at[(others, ALL) + piece_a], first_a + d - 1)
        arrived(b.w.at[(others, ALL) + piece_b], first_b + d - 1)
    row_a = (tile16(y), LOW)
    row_b = (tile16(x), HIGH)
    for d in range(1, 4):
        part_a = b.w.at[(others, ALL) + row_a]
        part_b = b.w.at[(others, ALL) + row_b]
        push(part_a, part_a, second_a + d - 1, at_y(d))
        push(part_b, part_b, second_b + d - 1, at_x(d))

    for d in range(1, 4):
        arrived(mine, mate_sem + d - 1)
    for t, place in enumerate((6, 7, 0, 1)):
        arrived(b.nodes.at[place], next_sem + t)

    def normalise(k, carry):
        hidden = dot(b.nodes[k], inputs.enc[...])
        centred = hidden - jnp.mean(hidden, axis=1, keepdims=True)
        spread = jnp.mean(centred * centred, axis=1, keepdims=True)
        b.normed[tile128(k), :] = (centred * lax.rsqrt(spread + 1e-05)).astype(BF16)
        return carry

    lax.fori_loop(0, 8, normalise, 0)

    for d in range(1, 4):
        arrived(b.w.at[(others, ALL) + row_a], second_a + d - 1)
        arrived(b.w.at[(others, ALL) + row_b], second_b + d - 1)
        arrived(b.cot.at[r], cot_sem + d - 1)

    sems_1 = [take(6) for _ in range(4)]
    sems_2 = [take(6) for _ in range(4)]

    def plane_first(c):
        for d in range(1, 4):
            to_y, to_x = lax.rem(y + d, 4), lax.rem(x + d, 4)
            push(b.grads.at[c, :, tile16(to_y), LOW], b.in_a1.at[c, d - 1], sems_1[c] + d - 1, at_y(d))
            push(b.grads.at[c, :, tile16(to_x), HIGH], b.in_b1.at[c, d - 1], sems_1[c] + 2 + d, at_x(d))

    def plane_second(c):
        for d in range(1, 4):
            arrived(b.in_a1.at[c, d - 1], sems_1[c] + d - 1)
            arrived(b.in_b1.at[c, d - 1], sems_1[c] + 2 + d)
        sum_a = b.grads[c, :, tile16(y), LOW].astype(F32)
        sum_b = b.grads[c, :, tile16(x), HIGH].astype(F32)
        for d in range(3):
            sum_a += b.in_a1[c, d].astype(F32)
            sum_b += b.in_b1[c, d].astype(F32)
        b.sum_a1[c] = sum_a.astype(BF16)
        b.sum_b1[c] = sum_b.astype(BF16)
        for d in range(1, 4):
            to_y, to_x = lax.rem(y + d, 4), lax.rem(x + d, 4)
            push(b.sum_a1.at[c, :, :, tile128(to_x)], b.in_a2.at[c, d - 1], sems_2[c] + d - 1, at_x(d))
            push(b.sum_b1.at[c, :, :, tile128(to_y)], b.in_b2.at[c, d - 1], sems_2[c] + 2 + d, at_y(d))

    def plane_last(c):
        for d in range(1, 4):
            arrived(b.in_a2.at[c, d - 1], sems_2[c] + d - 1)
            arrived(b.in_b2.at[c, d - 1], sems_2[c] + 2 + d)
        sum_a = b.sum_a1[c, :, :, tile128(x)].astype(F32)
        sum_b = b.sum_b1[c, :, :, tile128(y)].astype(F32)
        for d in range(3):
            sum_a += b.in_a2[c, d].astype(F32)
            sum_b += b.in_b2[c, d].astype(F32)
        b.plane[:, c, 0] = sum_a.astype(BF16)
        b.plane[:, c, 1] = sum_b.astype(BF16)

    part_sem = take(3)

    def after_forward():
        for c in (3, 2):
            plane_first(c)
        for d in range(1, 4):
            push(b.part.at[lax.rem(r + d, 4)], b.part_in.at[d - 1], part_sem + d - 1, mate(d))

    attention(grp, b.normed, b.w, b.cot, b.grads, b.part, s, after_forward)
    for c in (0, 1):
        plane_first(c)
    for c in (3, 2, 0, 1):
        plane_second(c)
    for c in (3, 2, 0, 1):
        plane_last(c)

    column_sem = take(7)
    for d in range(1, 8):
        there = lax.div(lax.rem(g + 4 * d, 32), 16)
        push(b.plane.at[SHARD_AT[d], pl.ds(there * 2, 2)], b.in_z.at[d - 1], column_sem + d - 1, at_col(g + 4 * d))

    out = dot(b.nodes[r + 2], inputs.enc[...]) + b.part[r].astype(F32)
    for d in range(3):
        arrived(b.part_in.at[d], part_sem + d)
        out += b.part_in[d].astype(F32)
    layer_out[0] = out.astype(BF16)

    total = b.plane[0, pl.ds(hi * 2, 2)].astype(F32)
    for d in range(7):
        arrived(b.in_z.at[d], column_sem + d)
        total += b.in_z[d].astype(F32)
    b.total[pl.ds(hi * 2, 2)] = total.astype(BF16)
    far_sem = take()
    half = b.total.at[pl.ds(hi * 2, 2)]
    push(half, half, far_sem, at_col(g + 16))
    arrived(b.total.at[pl.ds(2 - hi * 2, 2)], far_sem)

    b.gathered[:, piece_a[0], piece_a[1]] = b.total[:, 0]
    b.gathered[:, piece_b[0], piece_b[1]] = b.total[:, 1]
    last_1, last_2 = take(6), take(6)
    for d in range(1, 4):
        part_a, part_b = b.gathered.at[(ALL,) + piece_a], b.gathered.at[(ALL,) + piece_b]
        push(part_a, part_a, last_1 + d - 1, at_x(d))
        push(part_b, part_b, last_1 + 2 + d, at_y(d))
    for d in range(1, 4):
        arrived(b.gathered.at[(ALL,) + piece_a], last_1 + d - 1)
        arrived(b.gathered.at[(ALL,) + piece_b], last_1 + 2 + d)
    for d in range(1, 4):
        part_a, part_b = b.gathered.at[(ALL,) + row_a], b.gathered.at[(ALL,) + row_b]
        push(part_a, part_a, last_2 + d - 1, at_y(d))
        push(part_b, part_b, last_2 + 2 + d, at_x(d))
    for d in range(1, 4):
        arrived(b.gathered.at[(ALL,) + row_a], last_2 + d - 1)
        arrived(b.gathered.at[(ALL,) + row_b], last_2 + 2 + d)
    grad_qkv[...] = b.gathered[0:3].astype(F32)
    grad_out[...] = b.gathered[3].astype(F32)
    for copy in started:
        copy.wait_send()
    assert used[0] <= SEMS and len(started) <= SEMS


def on_device(
    grid_fields, edge_grid, edge_count, edge_weight, enc_weight, qkv_weight, out_weight, cotangent
):
    vmem, anywhere = pl.BlockSpec(memory_space=pltpu.VMEM), pl.BlockSpec(memory_space=pl.ANY)
    return pl.pallas_call(
        step_kernel,
        out_shape=(
            jax.ShapeDtypeStruct((1, 128, 1024), BF16),
            jax.ShapeDtypeStruct((3, 64, 1024), F32),
            jax.ShapeDtypeStruct((64, 1024), F32),
        ),
        in_specs=[anywhere, vmem, vmem, vmem, vmem, anywhere, anywhere, anywhere],
        out_specs=(vmem, vmem, vmem),
        scratch_shapes=[
            *EXCHANGE.values(),
            *ATTENTION.values(),
            pltpu.SemaphoreType.DMA((SEMS,)),
            pltpu.SemaphoreType.DMA((SEMS,)),
            pltpu.SemaphoreType.DMA((4,)),
        ],
        compiler_params=pltpu.CompilerParams(
            collective_id=0, has_side_effects=True, vmem_limit_bytes=56 * 1024 * 1024
        ),
    )(
        grid_fields.reshape(GRID_DEV, 128),
        edge_grid,
        edge_count.reshape(1, 128),
        edge_weight,
        enc_weight,
        qkv_weight,
        out_weight,
        cotangent.reshape(128, 1024),
    )


def solution(mesh):
    placed = (
        P("member", "mp", None),
        P("mp", None),
        P("mp"),
        P("mp", None),
        P(),
        P(None, "mp", None),
        P("mp", None),
        P("member", "mp", None),
    )
    return jax.shard_map(
        on_device,
        mesh=mesh,
        in_specs=placed,
        out_specs=(P("member", "mp", None), P(None, "mp", None), P("mp", None)),
        check_vma=False,
    )
```

time: 1110 us -> 113 us (0.10)
  waiting for transfers between devices: 860 us -> 0 us
  Pallas kernels: 0 us -> 104 us
  local copies, waits for them, and re-layouts: 85.3 us -> 6.69 us
  matrix products: 65 us -> 0 us
  other arithmetic: 54.8 us -> 0 us
  loops' own time: 16.7 us -> 0 us
  between operations: 14 us -> 0.65 us
    psum x1 -> x0, waiting for transfers between devices: 549 us -> none  [on_device(): lax.psum(grad_qkv.astype(jnp.bfloat16), 'member').astype(jnp.float32)]
    all_gather x3 -> x0, waiting for transfers between devices: 307 us -> none  [the longest x1 116 us: on_device(): full_out = lax.all_gather(out_weight, 'mp', axis=0, tiled=True)]
    pallas_call x0 -> x1, Pallas kernels: none -> 104 us  [on_device(): pl.pallas_call(step_kernel, out_shape=(jax.ShapeDtypeStruct((1, 128, 1024...]
    dot_general x30 -> x0, matrix products: 65 us -> none  [the longest x12 29 us: one_block(): jnp.einsum('ihe,jhe->hij', query_block, key_block, preferred_element_type...]
    dynamic_update_slice x16 -> x0, other arithmetic: 27.7 us -> none  [window_attention(): stacked = lax.map(one_block, block_starts)]
    add_any x12 -> x0, local copies, waits for them, and re-layouts: 27.6 us -> none  [the longest x4 9.28 us: one_block(): lax.dynamic_slice_in_dim(value_padded, block_start, key_span, 0)]
    dynamic_slice x24 -> x0, local copies, waits for them, and re-layouts: 19.3 us -> none  [window_attention(): stacked = lax.map(one_block, block_starts)]
    dynamic_update_slice x20 -> x0, local copies, waits for them, and re-layouts: 19 us -> none  [window_attention(): stacked = lax.map(one_block, block_starts)]
  transfers between devices with their start and end apart: 7 -> 0, of which waited for: 5 -> 0; matrix products, arithmetic and copies ran while one was open for 3% -> 0% of each run, Pallas kernels for 0% -> 0%
where the time goes in v1:
time: 113 us; the launch traced here: 111 us
  Pallas kernels  104 us (92%)
  local copies, waits for them, and re-layouts  6.69 us (6%)
    pallas_call x1, Pallas kernels, on_device(): pl.pallas_call(step_kernel, out_shape=(jax.ShapeDtypeStruct((1, 128, 1024...  104 us
    unnamed x9, local copies, waits for them, and re-layouts  6.69 us

profile of v1, /device:TPU:6, one launch (start us, length us, event | category | flops | bytes accessed | tf_op | source)
XLA Modules:
  0.0 111.3 jit_solution(6042595742281007612)
XLA Ops:
  0.6 0.0 copy-start.1
  0.6 1.5 %copy.11.refs_1_ = s32[128,32]{1,0:T(8,128)} copy(s32[128,32]{0,1:T(8,128)} %param.9) | data formatting | bytes 32768 | tf_op args[1]
  2.1 0.0 copy-done.1
  2.1 0.7 copy.12.refs_3_
  2.8 104.0 %shard_map.103 = (bf16[1,128,1024]{2,1,0:T(8,128)(2,1)}, f32[3,64,1024]{2,1,0:T(8,128)}, f32[64,1024]{1,0:T(8,128)}) custom-call(bf16[1728,128]{1,0:T(8,128)(2,1)} %bitcast.3, s32[128,32]{1,0:T(8,128)} %copy.11.refs_1_, s32[1,128]{1,0:T(1,128)} %bitcast.5, f32[128,32]{1,0:T(8,128)} %copy.12.refs_3_, bf16[128,1024]{1,0:T(8,128)(2,1)} %refs_4_.1, ...), custom_call_target="tpu_custom_call" | custom-call | tf_op jit(solution)/shard_map/pallas_call | solution.py:482
  106.8 1.7 %copy.16 = bf16[1,128,1024]{2,1,0:T(8,128)(2,1)} copy(bf16[1,128,1024]{2,1,0:T(8,128)(2,1)} %get-tuple-element.6) | data formatting | bytes 524288
  108.5 0.0 copy-start
  108.5 2.1 %copy.17 = f32[3,64,1024]{2,1,0:T(8,128)} copy(f32[3,64,1024]{2,1,0:T(8,128)} %get-tuple-element.7) | data formatting | bytes 1572864
  110.6 0.0 copy-done
  110.6 0.7 copy.18
Async XLA Ops:
  0.6 1.5 %copy-start.1 = (f32[128,32]{0,1:T(8,128)S(1)}, f32[128,32]{0,1:T(8,128)}, u32[]{:S(2)}) copy-start(f32[128,32]{0,1:T(8,128)} %param.11) | copy-start | bytes 49156
  108.5 2.1 %copy-start = (f32[64,1024]{1,0:T(8,128)S(1)}, f32[64,1024]{1,0:T(8,128)}, u32[]{:S(2)}) copy-start(f32[64,1024]{1,0:T(8,128)} %get-tuple-element.8) | copy-start | bytes 786436

commit v2 on v1

--- a/solution.py
+++ b/solution.py
@@ -17,7 +17,6 @@
 BAND = 17 * 128
 KEYS = 768
 NT = (((1,), (1,)), ((), ()))
-SHARD_AT = {0: 0, 4: 0, 7: 1, 3: 1, 1: 2, 5: 2, 2: 3, 6: 3}
 
 
 def dot(a, b):
@@ -41,7 +40,8 @@
         weights=pltpu.VMEM((8, KEYS, 256), BF16),
         row_d=pltpu.VMEM((8, 1, 256), F32),
         d_att_z=pltpu.VMEM((8, 128, 256), BF16),
-        att_t=pltpu.VMEM((256, 512), F32),
+        att_t=pltpu.VMEM((256, 512), BF16),
+        att=pltpu.VMEM((512, 256), BF16),
         d_query_t=pltpu.VMEM((256, 512), BF16),
         d_keys=pltpu.VMEM((1024, 256), F32),
         d_values=pltpu.VMEM((1024, 256), F32),
@@ -60,7 +60,7 @@
     lax.fori_loop(0, 4, tile, 0)
 
 
-def attention(grp, normed, w, cot, grads, part, s, after_forward):
+def attention(grp, normed, w, cot, grads, part, s, hooks):
     key_pos = lax.broadcasted_iota(jnp.int32, (KEYS, 256), 0)
     query_pos = lax.broadcasted_iota(jnp.int32, (KEYS, 256), 1)
     for qb in range(2):
@@ -73,7 +73,6 @@
     wq = w[:, 0].reshape(256, 1024)
     wk = w[:, 1].reshape(256, 1024)
     wv = w[:, 2].reshape(256, 1024)
-    wo = w[:, 3].reshape(256, 1024)
 
     def project(t, carry):
         rows = pl.ds(pl.multiple_of(t * 256, 256), 256)
@@ -96,11 +95,19 @@
             pair = query_t[h // 2 * 128 : h // 2 * 128 + 128]
             keep = upper if h % 2 == 0 else ~upper
             s.query_tz[h, :, rows] = jnp.where(keep, pair, 0.0).astype(BF16)
+        return carry
+
+    lax.fori_loop(0, 2, project_own, 0)
+    hooks.before_out()
+    wo = w[:, 3].reshape(256, 1024)
+
+    def project_cot(t, carry):
+        rows = pl.ds(pl.multiple_of(t * 256, 256), 256)
         cot_rows = cot[pl.ds(t * 2, 2)].reshape(256, 1024)
         s.d_att_t[:, rows] = dot_nt(wo, cot_rows).astype(BF16)
         return carry
 
-    lax.fori_loop(0, 2, project_own, 0)
+    lax.fori_loop(0, 2, project_cot, 0)
 
     def place(i):
         pair, qb = lax.div(i, 2), lax.rem(i, 2)
@@ -115,7 +122,7 @@
     def forward(i, carry):
         pair, qb, key_rows, lanes, cols = place(i)
         key_block = s.keys[key_rows, lanes]
-        all_weights, scaled = [], []
+        all_weights, scaled, outs = [], [], []
         for hh in range(2):
             scores = dot(key_block, s.query_tz[pair * 2 + hh, :, cols]) + s.bias[qb]
             weight = jnp.exp2(scores - jnp.max(scores, axis=0, keepdims=True))
@@ -127,8 +134,10 @@
             out = dot(s.values_t[rows, key_rows], weight) * inverse
             d_out = s.d_att_t[rows, cols].astype(F32)
             s.row_d[i * 2 + hh] = jnp.sum(d_out * out, axis=0, keepdims=True) * inverse
-            s.att_t[rows, cols] = out
+            s.att_t[rows, cols] = out.astype(BF16)
+            outs.append(out)
             scaled.append(d_out * inverse)
+        s.att[cols, lanes] = jnp.concatenate(outs, axis=0).T.astype(BF16)
         both = jnp.concatenate(scaled, axis=0)
         upper = lax.broadcasted_iota(jnp.int32, (128, 256), 0) < 64
         s.d_att_z[i * 2] = jnp.where(upper, both, 0.0).astype(BF16)
@@ -143,19 +152,19 @@
     lax.fori_loop(0, 4, forward, 0)
 
     def project_out(t, carry):
-        rows = pl.ds(pl.multiple_of(t * 128, 128), 128)
-        attended = s.att_t[:, rows].T.astype(BF16)
-        part[t] = dot(attended, wo).astype(BF16)
+        cols = pl.ds(pl.multiple_of(t * 256, 256), 256)
+        product = dot(s.att[...], w[:, 3, :, cols].reshape(256, 256)).astype(BF16)
+        for k in range(4):
+            part[k, :, cols] = product[k * 128 : (k + 1) * 128]
         return carry
 
     lax.fori_loop(0, 4, project_out, 0)
-    s.left[:, 0:512] = s.att_t[...].astype(BF16)
-    weight_grad(
-        grads, 3, lambda: s.left[:, 0:512], lambda cols: cot[:, :, cols].reshape(512, 256)
-    )
+    hooks.have_part()
+    weight_grad(grads, 3, lambda: s.att_t[...], lambda cols: cot[:, :, cols].reshape(512, 256))
+    hooks.have_grad(3)
     s.left[...] = s.d_values[...].T.astype(BF16)
     weight_grad(grads, 2, lambda: s.left[...], lambda cols: normed[:, cols])
-    after_forward()
+    hooks.have_grad(2)
 
     def backward(i, carry):
         pair, qb, key_rows, lanes, cols = place(i)
@@ -173,9 +182,12 @@
         return carry
 
     lax.fori_loop(0, 4, backward, 0)
+    hooks.after_backward()
     weight_grad(grads, 0, lambda: s.d_query_t[...], lambda cols: normed[256:768, cols])
+    hooks.have_grad(0)
     s.left[...] = s.d_keys[...].T.astype(BF16)
     weight_grad(grads, 1, lambda: s.left[...], lambda cols: normed[:, cols])
+    hooks.have_grad(1)
 
 
 class Names:
@@ -202,23 +214,41 @@
         in_a2=pltpu.VMEM((4, 3, 4, 16, 128), BF16),
         in_b2=pltpu.VMEM((4, 3, 4, 16, 128), BF16),
         plane=pltpu.VMEM((4, 4, 2, 16, 128), BF16),
-        in_z=pltpu.VMEM((7, 2, 2, 16, 128), BF16),
-        total=pltpu.VMEM((4, 2, 16, 128), BF16),
+        in_z=pltpu.VMEM((2, 4, 2, 16, 128), BF16),
+        in_z4=pltpu.VMEM((2, 4, 16, 128), BF16),
+        half_sum=pltpu.VMEM((4, 2, 16, 128), BF16),
+        far=pltpu.VMEM((4, 2, 16, 128), BF16),
         gathered=pltpu.VMEM((4, 64, 1024), BF16),
+        out=pltpu.VMEM((128, 1024), BF16),
+        edge=pltpu.VMEM((32, 128), jnp.int32),
+        count=pltpu.VMEM((1, 128), jnp.int32),
+        edge_w=pltpu.VMEM((32, 128), F32),
+        enc=pltpu.VMEM((128, 1024), BF16),
+        index=pltpu.VMEM((128, 32), jnp.int32),
     )
 
 
 EXCHANGE = exchange_scratch()
 ATTENTION = attention_scratch()
 SEMS = 128
+ALL = slice(None)
+LOW, HIGH = pl.ds(0, 512), pl.ds(512, 512)
+
+
+def tile16(k):
+    return pl.ds(pl.multiple_of(k * 16, 16), 16)
+
+
+def tile128(k):
+    return pl.ds(pl.multiple_of(k * 128, 128), 128)
 
 
 def step_kernel(*refs):
     inputs = Names(("grid", "edge", "count", "edge_w", "enc", "wqkv", "wo", "cot"), refs[:8])
-    layer_out, grad_qkv, grad_out = refs[8:11]
-    b = Names(tuple(EXCHANGE), refs[11 : 11 + len(EXCHANGE)])
-    s = Names(tuple(ATTENTION), refs[11 + len(EXCHANGE) : 11 + len(EXCHANGE) + len(ATTENTION)])
-    send_sem, recv_sem, local_sem = refs[11 + len(EXCHANGE) + len(ATTENTION) :]
+    layer_out, weight_grads = refs[8:10]
+    b = Names(tuple(EXCHANGE), refs[10 : 10 + len(EXCHANGE)])
+    s = Names(tuple(ATTENTION), refs[10 + len(EXCHANGE) : 10 + len(EXCHANGE) + len(ATTENTION)])
+    send_sem, recv_sem, local_sem = refs[10 + len(EXCHANGE) + len(ATTENTION) :]
 
     member, mp = lax.axis_index("member"), lax.axis_index("mp")
     x, hi, y = lax.div(member, 8), lax.rem(lax.div(member, 4), 2), lax.rem(member, 4)
@@ -238,7 +268,7 @@
     def mate(d):
         return at_col(g - r + lax.rem(r + d, 4))
 
-    started, used = [], [0]
+    started, used, local = [], [0], [0]
 
     def take(n=1):
         used[0] += n
@@ -259,54 +289,56 @@
     def arrived(dst, recv):
         pltpu.make_async_copy(dst, dst, recv_sem.at[recv]).wait()
 
-    def tile16(k):
-        return pl.ds(pl.multiple_of(k * 16, 16), 16)
-
-    def tile128(k):
-        return pl.ds(pl.multiple_of(k * 128, 128), 128)
-
-    LOW, HIGH = pl.ds(0, 512), pl.ds(512, 512)
+    def here(src, dst):
+        copy = pltpu.make_async_copy(src, dst, local_sem.at[local[0]])
+        local[0] += 1
+        copy.start()
+        return copy
 
     barrier = pltpu.get_barrier_semaphore()
-    sources = [at_col(g + 4 * d) for d in range(1, 8)]
+    sources = [at_col(g + 4 * d) for d in (1, -1, 2, -2)]
     sources += [at_x(d) for d in range(1, 4)] + [at_y(d) for d in range(1, 4)]
     sources += [mate(d) for d in range(1, 4)]
     sources += [at_col(g - r + d) for d in (-2, -1, 4, 5)]
     for device in sources:
         pl.semaphore_signal(barrier, inc=1, device_id=device, device_id_type=MESH)
-    own_grid = pltpu.make_async_copy(inputs.grid, b.ext.at[pl.ds(GRID_DEV, GRID_DEV)], local_sem.at[0])
-    own_w = pltpu.make_async_copy(inputs.wqkv, b.w.at[0, pl.ds(0, 3)], local_sem.at[1])
-    own_wo = pltpu.make_async_copy(inputs.wo, b.w.at[0, 3], local_sem.at[2])
-    own_cot = pltpu.make_async_copy(inputs.cot, b.cot.at[r], local_sem.at[3])
-    for copy in (own_grid, own_w, own_wo, own_cot):
-        copy.start()
+    own_w = here(inputs.wqkv, b.w.at[0, pl.ds(0, 3)])
+    own_wo = here(inputs.wo, b.w.at[0, 3])
+    edges = [here(getattr(inputs, n), getattr(b, n)) for n in ("edge", "count", "edge_w")]
+    own_enc = here(inputs.enc, b.enc)
+    own_grid = here(inputs.grid, b.ext.at[pl.ds(GRID_DEV, GRID_DEV)])
+    own_cot = here(inputs.cot, b.cot.at[r])
     pl.semaphore_wait(barrier, len(sources))
+
+    own_w.wait()
+    own_wo.wait()
+    piece_a = (tile16(y), tile128(x))
+    piece_b = (tile16(x), tile128(y + 4))
+    z_sem = take(6)
+    for n, (j, off_a, off_b) in enumerate(((1, 4, 4), (2, -4, -4), (3, 8, -8))):
+        push(b.w.at[(0, ALL) + piece_a], b.w.at[(j, ALL) + piece_a], z_sem + n, at_col(g + off_a))
+        push(b.w.at[(0, ALL) + piece_b], b.w.at[(j, ALL) + piece_b], z_sem + 3 + n, at_col(g + off_b))
 
     left_rows, right_rows = pl.ds(0, GRID_DEV), pl.ds(2 * GRID_DEV, GRID_DEV)
     grid_sem = take(2)
     push(inputs.grid, b.ext.at[left_rows], grid_sem, at_col(g + 1))
     push(inputs.grid, b.ext.at[right_rows], grid_sem + 1, at_col(g - 1))
 
-    own_w.wait()
-    own_wo.wait()
-    piece_a = (tile16(y), tile128(x))
-    piece_b = (tile16(x), tile128(y + 4))
-    ALL = slice(None)
-    z_sem = take(6)
-    for n, (j, off) in enumerate(((1, 4), (2, -4), (3, 8))):
-        push(b.w.at[(0, ALL) + piece_a], b.w.at[(j, ALL) + piece_a], z_sem + n, at_col(g + off))
-        push(b.w.at[(0, ALL) + piece_b], b.w.at[(j, ALL) + piece_b], z_sem + 3 + n, at_col(g + off))
-
     b.place[...] = jnp.zeros_like(b.place)
     b.ext[pl.ds(3 * GRID_DEV, EXT - 3 * GRID_DEV), :] = jnp.zeros((EXT - 3 * GRID_DEV, 128), BF16)
-    counts = jnp.broadcast_to(inputs.count[...].astype(F32), (128, 128)).T[:, :32]
-    slot = lax.broadcasted_iota(jnp.int32, (128, 32), 1).astype(F32)
-    b.coef[...] = jnp.where(slot < counts, inputs.edge_w[...], 0.0)
+    for copy in edges:
+        copy.wait()
+    slot = lax.broadcasted_iota(jnp.int32, (32, 128), 0)
+    coef = jnp.where(slot < b.count[...], b.edge_w[...], 0.0)
+    index = (b.edge[...] - (mp - 1) * GRID_DEV).astype(F32)
+    both = jnp.concatenate([coef, index, jnp.zeros((64, 128), F32)], axis=0).T
+    b.coef[...] = both[:, 0:32]
+    b.index[...] = both[:, 32:64].astype(jnp.int32)
 
     def build(k, carry):
         rows = tile16(k)
         start = pl.multiple_of(lax.div(862 + 216 * k, 128) * 128, 128)
-        index = inputs.edge[rows, :] - ((mp - 1) * GRID_DEV + start)
+        index = b.index[rows, :] - start
         coef = b.coef[rows, :]
         lane = lax.broadcasted_iota(jnp.int32, (16, BAND), 1)
         total = jnp.zeros((16, BAND), F32)
@@ -318,7 +350,6 @@
     lax.fori_loop(0, 8, build, 0)
 
     others = pl.ds(1, 3)
-    w_all = b.w.at[others]
     for n in range(3):
         arrived(b.w.at[(n + 1, ALL) + piece_a], z_sem + n)
         arrived(b.w.at[(n + 1, ALL) + piece_b], z_sem + 3 + n)
@@ -336,35 +367,47 @@
     b.nodes[pl.ds(r + 2, 1)] = node_in[None]
     mine = b.nodes.at[r + 2]
     mate_sem, next_sem = take(3), take(4)
+    near = jnp.where(r < 2, g - r - 4, g - r + 4)
     for d in range(1, 4):
         push(mine, mine, mate_sem + d - 1, mate(d))
-    near = jnp.where(r < 2, g - r - 4, g - r + 4)
     for t in range(4):
         push(mine, b.nodes.at[lax.rem(r + 6, 8)], next_sem + r, at_col(near + t))
-    own_cot.wait()
-    cot_sem = take(3)
-    for d in range(1, 4):
-        push(b.cot.at[r], b.cot.at[r], cot_sem + d - 1, mate(d))
-
-    second_a, second_b = take(3), take(3)
+
     for d in range(1, 4):
         arrived(b.w.at[(others, ALL) + piece_a], first_a + d - 1)
         arrived(b.w.at[(others, ALL) + piece_b], first_b + d - 1)
     row_a = (tile16(y), LOW)
     row_b = (tile16(x), HIGH)
-    for d in range(1, 4):
-        part_a = b.w.at[(others, ALL) + row_a]
-        part_b = b.w.at[(others, ALL) + row_b]
-        push(part_a, part_a, second_a + d - 1, at_y(d))
-        push(part_b, part_b, second_b + d - 1, at_x(d))
+    QKV, OUT = pl.ds(0, 3), pl.ds(3, 1)
+    second = {}
+    for kinds, name in ((QKV, "qkv"), (OUT, "out")):
+        second[name] = take(6)
+        for d in range(1, 4):
+            part_a = b.w.at[(others, kinds) + row_a]
+            part_b = b.w.at[(others, kinds) + row_b]
+            push(part_a, part_a, second[name] + d - 1, at_y(d))
+            push(part_b, part_b, second[name] + 2 + d, at_x(d))
+
+    def wait_second(kinds, name):
+        for d in range(1, 4):
+            arrived(b.w.at[(others, kinds) + row_a], second[name] + d - 1)
+            arrived(b.w.at[(others, kinds) + row_b], second[name] + 2 + d)
+
+    own_cot.wait()
+    cot_sem = take(3)
+    sibling = r + 1 - 2 * lax.rem(r, 2)
+    across = lax.rem(r + 2, 4)
+    push(b.cot.at[r], b.cot.at[r], cot_sem, at_col(g - r + across))
+    push(b.cot.at[r], b.cot.at[r], cot_sem + 1, at_col(g - r + sibling))
 
     for d in range(1, 4):
         arrived(mine, mate_sem + d - 1)
     for t, place in enumerate((6, 7, 0, 1)):
         arrived(b.nodes.at[place], next_sem + t)
+    own_enc.wait()
 
     def normalise(k, carry):
-        hidden = dot(b.nodes[k], inputs.enc[...])
+        hidden = dot(b.nodes[k], b.enc[...])
         centred = hidden - jnp.mean(hidden, axis=1, keepdims=True)
         spread = jnp.mean(centred * centred, axis=1, keepdims=True)
         b.normed[tile128(k), :] = (centred * lax.rsqrt(spread + 1e-05)).astype(BF16)
@@ -372,13 +415,13 @@
 
     lax.fori_loop(0, 8, normalise, 0)
 
-    for d in range(1, 4):
-        arrived(b.w.at[(others, ALL) + row_a], second_a + d - 1)
-        arrived(b.w.at[(others, ALL) + row_b], second_b + d - 1)
-        arrived(b.cot.at[r], cot_sem + d - 1)
+    arrived(b.cot.at[across], cot_sem)
+    push(b.cot.at[across], b.cot.at[across], cot_sem + 2, at_col(g - r + sibling))
+    wait_second(QKV, "qkv")
 
     sems_1 = [take(6) for _ in range(4)]
     sems_2 = [take(6) for _ in range(4)]
+    part_sem = take(3)
 
     def plane_first(c):
         for d in range(1, 4):
@@ -414,100 +457,156 @@
         b.plane[:, c, 0] = sum_a.astype(BF16)
         b.plane[:, c, 1] = sum_b.astype(BF16)
 
-    part_sem = take(3)
-
-    def after_forward():
-        for c in (3, 2):
+    class Column:
+        def __init__(self, first):
+            self.c = pl.ds(first, 2)
+            self.near, self.far, self.one, self.two = take(4), take(), take(6), take(6)
+
+        def to_owners(self):
+            c = self.c
+            push(b.plane.at[1, c], b.in_z.at[0, c], self.near, at_col(g - 4))
+            push(b.plane.at[2, c], b.in_z.at[1, c], self.near + 1, at_col(g + 4))
+            push(b.plane.at[3, c, 0], b.in_z4.at[0, c], self.near + 2, at_col(g + 8))
+            push(b.plane.at[3, c, 1], b.in_z4.at[1, c], self.near + 3, at_col(g - 8))
+
+        def to_far(self):
+            c = self.c
+            for n in range(2):
+                arrived(b.in_z.at[n, c], self.near + n)
+                arrived(b.in_z4.at[n, c], self.near + 2 + n)
+            for n in range(2):
+                total = b.plane[0, c, n].astype(F32) + b.in_z4[n, c].astype(F32)
+                total += b.in_z[0, c, n].astype(F32) + b.in_z[1, c, n].astype(F32)
+                b.half_sum[c, n] = total.astype(BF16)
+            push(b.half_sum.at[c], b.far.at[c], self.far, at_col(g + 16))
+
+        def to_plane(self):
+            c = self.c
+            arrived(b.far.at[c], self.far)
+            total = (b.half_sum[c].astype(F32) + b.far[c].astype(F32)).astype(BF16)
+            b.gathered[c, piece_a[0], piece_a[1]] = total[:, 0]
+            b.gathered[c, piece_b[0], piece_b[1]] = total[:, 1]
+            for d in range(1, 4):
+                part_a, part_b = b.gathered.at[(c,) + piece_a], b.gathered.at[(c,) + piece_b]
+                push(part_a, part_a, self.one + d - 1, at_x(d))
+                push(part_b, part_b, self.one + 2 + d, at_y(d))
+
+        def to_rest(self):
+            c = self.c
+            for d in range(1, 4):
+                arrived(b.gathered.at[(c,) + piece_a], self.one + d - 1)
+                arrived(b.gathered.at[(c,) + piece_b], self.one + 2 + d)
+            for d in range(1, 4):
+                part_a, part_b = b.gathered.at[(c,) + row_a], b.gathered.at[(c,) + row_b]
+                push(part_a, part_a, self.two + d - 1, at_y(d))
+                push(part_b, part_b, self.two + 2 + d, at_x(d))
+
+        def finish(self):
+            c = self.c
+            for d in range(1, 4):
+                arrived(b.gathered.at[(c,) + row_a], self.two + d - 1)
+                arrived(b.gathered.at[(c,) + row_b], self.two + 2 + d)
+            return here(b.gathered.at[c], weight_grads.at[c])
+
+    early, late = Column(2), Column(0)
+
+    class Hooks:
+        def before_out(self):
+            wait_second(OUT, "out")
+            arrived(b.cot.at[sibling], cot_sem + 1)
+            arrived(b.cot.at[lax.rem(sibling + 2, 4)], cot_sem + 2)
+
+        def have_part(self):
+            for d in range(1, 4):
+                push(b.part.at[lax.rem(r + d, 4)], b.part_in.at[d - 1], part_sem + d - 1, mate(d))
+
+        def have_grad(self, c):
             plane_first(c)
-        for d in range(1, 4):
-            push(b.part.at[lax.rem(r + d, 4)], b.part_in.at[d - 1], part_sem + d - 1, mate(d))
-
-    attention(grp, b.normed, b.w, b.cot, b.grads, b.part, s, after_forward)
-    for c in (0, 1):
-        plane_first(c)
-    for c in (3, 2, 0, 1):
-        plane_second(c)
-    for c in (3, 2, 0, 1):
-        plane_last(c)
-
-    column_sem = take(7)
-    for d in range(1, 8):
-        there = lax.div(lax.rem(g + 4 * d, 32), 16)
-        push(b.plane.at[SHARD_AT[d], pl.ds(there * 2, 2)], b.in_z.at[d - 1], column_sem + d - 1, at_col(g + 4 * d))
-
-    out = dot(b.nodes[r + 2], inputs.enc[...]) + b.part[r].astype(F32)
+
+        def after_backward(self):
+            plane_second(3)
+            plane_second(2)
+
+    attention(grp, b.normed, b.w, b.cot, b.grads, b.part, s, Hooks())
+
+    plane_last(3)
+    plane_last(2)
+    early.to_owners()
+    out = dot(b.nodes[r + 2], b.enc[...]) + b.part[r].astype(F32)
     for d in range(3):
         arrived(b.part_in.at[d], part_sem + d)
         out += b.part_in[d].astype(F32)
-    layer_out[0] = out.astype(BF16)
-
-    total = b.plane[0, pl.ds(hi * 2, 2)].astype(F32)
-    for d in range(7):
-        arrived(b.in_z.at[d], column_sem + d)
-        total += b.in_z[d].astype(F32)
-    b.total[pl.ds(hi * 2, 2)] = total.astype(BF16)
-    far_sem = take()
-    half = b.total.at[pl.ds(hi * 2, 2)]
-    push(half, half, far_sem, at_col(g + 16))
-    arrived(b.total.at[pl.ds(2 - hi * 2, 2)], far_sem)
-
-    b.gathered[:, piece_a[0], piece_a[1]] = b.total[:, 0]
-    b.gathered[:, piece_b[0], piece_b[1]] = b.total[:, 1]
-    last_1, last_2 = take(6), take(6)
-    for d in range(1, 4):
-        part_a, part_b = b.gathered.at[(ALL,) + piece_a], b.gathered.at[(ALL,) + piece_b]
-        push(part_a, part_a, last_1 + d - 1, at_x(d))
-        push(part_b, part_b, last_1 + 2 + d, at_y(d))
-    for d in range(1, 4):
-        arrived(b.gathered.at[(ALL,) + piece_a], last_1 + d - 1)
-        arrived(b.gathered.at[(ALL,) + piece_b], last_1 + 2 + d)
-    for d in range(1, 4):
-        part_a, part_b = b.gathered.at[(ALL,) + row_a], b.gathered.at[(ALL,) + row_b]
-        push(part_a, part_a, last_2 + d - 1, at_y(d))
-        push(part_b, part_b, last_2 + 2 + d, at_x(d))
-    for d in range(1, 4):
-        arrived(b.gathered.at[(ALL,) + row_a], last_2 + d - 1)
-        arrived(b.gathered.at[(ALL,) + row_b], last_2 + 2 + d)
-    grad_qkv[...] = b.gathered[0:3].astype(F32)
-    grad_out[...] = b.gathered[3].astype(F32)
+    b.out[...] = out.astype(BF16)
+    results = [here(b.out, layer_out)]
+    plane_second(0)
+    plane_second(1)
+    early.to_far()
+    plane_last(0)
+    plane_last(1)
+    late.to_owners()
+    early.to_plane()
+    late.to_far()
+    early.to_rest()
+    late.to_plane()
+    results.append(early.finish())
+    late.to_rest()
+    results.append(late.finish())
+    for copy in results:
+        copy.wait()
     for copy in started:
         copy.wait_send()
-    assert used[0] <= SEMS and len(started) <= SEMS
+    assert used[0] <= SEMS and len(started) <= SEMS and local[0] <= 16
+
+
+def finish_kernel(layer_in, grads, layer_out, grad_qkv, grad_out):
+    layer_out[...] = layer_in[...]
+    grad_qkv[...] = grads[0:3].astype(F32)
+    grad_out[...] = grads[3].astype(F32)
 
 
 def on_device(
     grid_fields, edge_grid, edge_count, edge_weight, enc_weight, qkv_weight, out_weight, cotangent
 ):
     vmem, anywhere = pl.BlockSpec(memory_space=pltpu.VMEM), pl.BlockSpec(memory_space=pl.ANY)
-    return pl.pallas_call(
+    layer_out, grads = pl.pallas_call(
         step_kernel,
         out_shape=(
-            jax.ShapeDtypeStruct((1, 128, 1024), BF16),
-            jax.ShapeDtypeStruct((3, 64, 1024), F32),
-            jax.ShapeDtypeStruct((64, 1024), F32),
+            jax.ShapeDtypeStruct((128, 1024), BF16),
+            jax.ShapeDtypeStruct((4, 64, 1024), BF16),
         ),
-        in_specs=[anywhere, vmem, vmem, vmem, vmem, anywhere, anywhere, anywhere],
-        out_specs=(vmem, vmem, vmem),
+        in_specs=[anywhere] * 8,
+        out_specs=(anywhere, anywhere),
         scratch_shapes=[
             *EXCHANGE.values(),
             *ATTENTION.values(),
             pltpu.SemaphoreType.DMA((SEMS,)),
             pltpu.SemaphoreType.DMA((SEMS,)),
-            pltpu.SemaphoreType.DMA((4,)),
+            pltpu.SemaphoreType.DMA((16,)),
         ],
         compiler_params=pltpu.CompilerParams(
             collective_id=0, has_side_effects=True, vmem_limit_bytes=56 * 1024 * 1024
         ),
     )(
         grid_fields.reshape(GRID_DEV, 128),
-        edge_grid,
+        edge_grid.T,
         edge_count.reshape(1, 128),
-        edge_weight,
+        edge_weight.T,
         enc_weight,
         qkv_weight,
         out_weight,
         cotangent.reshape(128, 1024),
     )
+    layer_out, grad_qkv, grad_out = pl.pallas_call(
+        finish_kernel,
+        out_shape=(
+            jax.ShapeDtypeStruct((128, 1024), BF16),
+            jax.ShapeDtypeStruct((3, 64, 1024), F32),
+            jax.ShapeDtypeStruct((64, 1024), F32),
+        ),
+        in_specs=[vmem, vmem],
+        out_specs=(vmem, vmem, vmem),
+    )(layer_out, grads)
+    return layer_out[None], grad_qkv, grad_out
 
 
 def solution(mesh):

time: 113 us -> 93.3 us (0.83); the launches traced: 111 us -> 93.1 us
  Pallas kernels: 104 us -> 92.5 us
  local copies, waits for them, and re-layouts: 6.69 us -> 0 us
    pallas_call x1 -> x2, Pallas kernels: 104 us -> 92.5 us  [the longest x1 90.2 us: on_device(): pl.pallas_call(step_kernel, out_shape=(jax.ShapeDtypeStruct((128, 1024),...]
    unnamed x9 -> x0, local copies, waits for them, and re-layouts: 6.69 us -> none
where the time goes in v2:
time: 93.3 us; the launch traced here: 93.1 us
  Pallas kernels  92.5 us (99%)
    pallas_call x1, Pallas kernels, on_device(): pl.pallas_call(step_kernel, out_shape=(jax.ShapeDtypeStruct((128, 1024),...  90.2 us
    pallas_call x1, Pallas kernels, on_device(): pl.pallas_call(finish_kernel, out_shape=(jax.ShapeDtypeStruct((128, 1024)...  2.24 us

profile of v2, /device:TPU:6, one launch (start us, length us, event | category | flops | bytes accessed | tf_op | source)
XLA Modules:
  0.0 93.1 jit_solution(16416575770676800849)
XLA Ops:
  0.6 90.2 %shard_map.103 = (bf16[128,1024]{1,0:T(8,128)(2,1)}, bf16[4,64,1024]{2,1,0:T(8,128)(2,1)}) custom-call(bf16[1728,128]{1,0:T(8,128)(2,1)} %bitcast.6, s32[32,128]{1,0:T(8,128)} %bitcast.8, s32[1,128]{1,0:T(1,128)} %bitcast.10, f32[32,128]{1,0:T(8,128)} %bitcast.9, bf16[128,1024]{1,0:T(8,128)(2,1)} %refs_4_.1, bf16[3,64,1024]{2,1,0:T(8,128)(2,1)} %refs_5_.1, ...), custom_call_target="tpu_custom_call" | custom-call | tf_op jit(solution)/shard_map/pallas_call | solution.py:571
  90.9 2.2 %shard_map.104 = (bf16[128,1024]{1,0:T(8,128)(2,1)}, f32[3,64,1024]{2,1,0:T(8,128)}, f32[64,1024]{1,0:T(8,128)}) custom-call(bf16[128,1024]{1,0:T(8,128)(2,1)} %get-tuple-element.8.layer_in, bf16[4,64,1024]{2,1,0:T(8,128)(2,1)} %get-tuple-element.9.grads), custom_call_target="tpu_custom_call" | custom-call | tf_op jit(solution)/shard_map/pallas_call | solution.py:599

commit v3 on v2

--- a/solution.py
+++ b/solution.py
@@ -17,6 +17,7 @@
 BAND = 17 * 128
 KEYS = 768
 NT = (((1,), (1,)), ((), ()))
+SHARD_AT = {1: 2, 2: 3, 3: 1, 4: 0, 5: 2, 6: 3, 7: 1}
 
 
 def dot(a, b):
@@ -57,7 +58,18 @@
             grads[c, j, :, cols] = product[j * 64 : (j + 1) * 64]
         return carry
 
-    lax.fori_loop(0, 4, tile, 0)
+    lax.fori_loop(0, 4, tile, 0, unroll=True)
+
+
+def project_attended(w, s, part):
+    def project_out(t, carry):
+        cols = pl.ds(pl.multiple_of(t * 256, 256), 256)
+        product = dot(s.att[...], w[:, 3, :, cols].reshape(256, 256)).astype(BF16)
+        for k in range(4):
+            part[k, :, cols] = product[k * 128 : (k + 1) * 128]
+        return carry
+
+    lax.fori_loop(0, 4, project_out, 0, unroll=True)
 
 
 def attention(grp, normed, w, cot, grads, part, s, hooks):
@@ -70,7 +82,6 @@
     s.d_keys[...] = jnp.zeros_like(s.d_keys)
     s.d_values[...] = jnp.zeros_like(s.d_values)
 
-    wq = w[:, 0].reshape(256, 1024)
     wk = w[:, 1].reshape(256, 1024)
     wv = w[:, 2].reshape(256, 1024)
 
@@ -83,7 +94,9 @@
         s.values_t[:, rows] = dot_nt(wv, block).astype(BF16)
         return carry
 
-    lax.fori_loop(0, 4, project, 0)
+    lax.fori_loop(0, 4, project, 0, unroll=True)
+    hooks.before_query()
+    wq = w[:, 0].reshape(256, 1024)
 
     def project_own(t, carry):
         rows = pl.ds(pl.multiple_of(t * 256, 256), 256)
@@ -97,7 +110,7 @@
             s.query_tz[h, :, rows] = jnp.where(keep, pair, 0.0).astype(BF16)
         return carry
 
-    lax.fori_loop(0, 2, project_own, 0)
+    lax.fori_loop(0, 2, project_own, 0, unroll=True)
     hooks.before_out()
     wo = w[:, 3].reshape(256, 1024)
 
@@ -107,7 +120,7 @@
         s.d_att_t[:, rows] = dot_nt(wo, cot_rows).astype(BF16)
         return carry
 
-    lax.fori_loop(0, 2, project_cot, 0)
+    lax.fori_loop(0, 2, project_cot, 0, unroll=True)
 
     def place(i):
         pair, qb = lax.div(i, 2), lax.rem(i, 2)
@@ -122,16 +135,19 @@
     def forward(i, carry):
         pair, qb, key_rows, lanes, cols = place(i)
         key_block = s.keys[key_rows, lanes]
-        all_weights, scaled, outs = [], [], []
+        scaled, outs = [], []
+        scores = [dot(key_block, s.query_tz[pair * 2 + hh, :, cols]) + s.bias[qb] for hh in range(2)]
+        tops = [jnp.max(v, axis=0, keepdims=True) for v in scores]
+        all_weights, inverses = [], []
         for hh in range(2):
-            scores = dot(key_block, s.query_tz[pair * 2 + hh, :, cols]) + s.bias[qb]
-            weight = jnp.exp2(scores - jnp.max(scores, axis=0, keepdims=True))
-            inverse = 1.0 / jnp.sum(weight, axis=0, keepdims=True)
-            weight = weight.astype(BF16)
-            s.weights[i * 2 + hh] = weight
-            all_weights.append(weight)
+            weight = jnp.exp2(scores[hh] - tops[hh])
+            inverses.append(1.0 / jnp.sum(weight, axis=0, keepdims=True))
+            all_weights.append(weight.astype(BF16))
+            s.weights[i * 2 + hh] = all_weights[hh]
+        for hh in range(2):
             rows = head_rows(pair, hh)
-            out = dot(s.values_t[rows, key_rows], weight) * inverse
+            inverse = inverses[hh]
+            out = dot(s.values_t[rows, key_rows], all_weights[hh]) * inverse
             d_out = s.d_att_t[rows, cols].astype(F32)
             s.row_d[i * 2 + hh] = jnp.sum(d_out * out, axis=0, keepdims=True) * inverse
             s.att_t[rows, cols] = out.astype(BF16)
@@ -149,22 +165,15 @@
         ) + dot(all_weights[1], jnp.where(low, 0.0, rows_form).astype(BF16))
         return carry
 
-    lax.fori_loop(0, 4, forward, 0)
-
-    def project_out(t, carry):
-        cols = pl.ds(pl.multiple_of(t * 256, 256), 256)
-        product = dot(s.att[...], w[:, 3, :, cols].reshape(256, 256)).astype(BF16)
-        for k in range(4):
-            part[k, :, cols] = product[k * 128 : (k + 1) * 128]
-        return carry
-
-    lax.fori_loop(0, 4, project_out, 0)
-    hooks.have_part()
+    lax.fori_loop(0, 4, forward, 0, unroll=True)
+
     weight_grad(grads, 3, lambda: s.att_t[...], lambda cols: cot[:, :, cols].reshape(512, 256))
     hooks.have_grad(3)
     s.left[...] = s.d_values[...].T.astype(BF16)
     weight_grad(grads, 2, lambda: s.left[...], lambda cols: normed[:, cols])
     hooks.have_grad(2)
+    project_attended(w, s, part)
+    hooks.have_part()
 
     def backward(i, carry):
         pair, qb, key_rows, lanes, cols = place(i)
@@ -181,8 +190,7 @@
         s.d_keys[key_rows, lanes] += d_keys * (1.0 / LOG2E)
         return carry
 
-    lax.fori_loop(0, 4, backward, 0)
-    hooks.after_backward()
+    lax.fori_loop(0, 4, backward, 0, unroll=True)
     weight_grad(grads, 0, lambda: s.d_query_t[...], lambda cols: normed[256:768, cols])
     hooks.have_grad(0)
     s.left[...] = s.d_keys[...].T.astype(BF16)
@@ -211,13 +219,10 @@
         in_b1=pltpu.VMEM((4, 3, 4, 16, 512), BF16),
         sum_a1=pltpu.VMEM((4, 4, 16, 512), BF16),
         sum_b1=pltpu.VMEM((4, 4, 16, 512), BF16),
-        in_a2=pltpu.VMEM((4, 3, 4, 16, 128), BF16),
-        in_b2=pltpu.VMEM((4, 3, 4, 16, 128), BF16),
+        in_a2=pltpu.VMEM((3, 4, 4, 16, 128), BF16),
+        in_b2=pltpu.VMEM((3, 4, 4, 16, 128), BF16),
         plane=pltpu.VMEM((4, 4, 2, 16, 128), BF16),
-        in_z=pltpu.VMEM((2, 4, 2, 16, 128), BF16),
-        in_z4=pltpu.VMEM((2, 4, 16, 128), BF16),
-        half_sum=pltpu.VMEM((4, 2, 16, 128), BF16),
-        far=pltpu.VMEM((4, 2, 16, 128), BF16),
+        in_z=pltpu.VMEM((8, 4, 2, 16, 128), BF16),
         gathered=pltpu.VMEM((4, 64, 1024), BF16),
         out=pltpu.VMEM((128, 1024), BF16),
         edge=pltpu.VMEM((32, 128), jnp.int32),
@@ -230,9 +235,10 @@
 
 EXCHANGE = exchange_scratch()
 ATTENTION = attention_scratch()
-SEMS = 128
+SEMS = 192
 ALL = slice(None)
 LOW, HIGH = pl.ds(0, 512), pl.ds(512, 512)
+QUERY, KV, OUT = pl.ds(0, 1), pl.ds(1, 2), pl.ds(3, 1)
 
 
 def tile16(k):
@@ -302,7 +308,7 @@
     sources += [at_col(g - r + d) for d in (-2, -1, 4, 5)]
     for device in sources:
         pl.semaphore_signal(barrier, inc=1, device_id=device, device_id_type=MESH)
-    own_w = here(inputs.wqkv, b.w.at[0, pl.ds(0, 3)])
+    own_qkv = here(inputs.wqkv, b.w.at[0, pl.ds(0, 3)])
     own_wo = here(inputs.wo, b.w.at[0, 3])
     edges = [here(getattr(inputs, n), getattr(b, n)) for n in ("edge", "count", "edge_w")]
     own_enc = here(inputs.enc, b.enc)
@@ -310,14 +316,27 @@
     own_cot = here(inputs.cot, b.cot.at[r])
     pl.semaphore_wait(barrier, len(sources))
 
-    own_w.wait()
-    own_wo.wait()
-    piece_a = (tile16(y), tile128(x))
-    piece_b = (tile16(x), tile128(y + 4))
-    z_sem = take(6)
+    piece_a, row_a = (tile16(y), tile128(x)), (tile16(y), LOW)
+    piece_b, row_b = (tile16(x), tile128(y + 4)), (tile16(x), HIGH)
+    others = pl.ds(1, 3)
+
+    def across(kinds, sems, first, second, at_first, at_second):
+        for d in range(1, 4):
+            part_a = b.w.at[(others, kinds) + first]
+            part_b = b.w.at[(others, kinds) + second]
+            push(part_a, part_a, sems + d - 1, at_first(d))
+            push(part_b, part_b, sems + 2 + d, at_second(d))
+
+    def across_arrived(kinds, sems, first, second):
+        for d in range(3):
+            arrived(b.w.at[(others, kinds) + first], sems + d)
+            arrived(b.w.at[(others, kinds) + second], sems + 3 + d)
+
+    w_one, w_two = take(12), take(6)
     for n, (j, off_a, off_b) in enumerate(((1, 4, 4), (2, -4, -4), (3, 8, -8))):
-        push(b.w.at[(0, ALL) + piece_a], b.w.at[(j, ALL) + piece_a], z_sem + n, at_col(g + off_a))
-        push(b.w.at[(0, ALL) + piece_b], b.w.at[(j, ALL) + piece_b], z_sem + 3 + n, at_col(g + off_b))
+        for m, off, piece in ((0, off_a, piece_a), (3, off_b, piece_b)):
+            push(inputs.wqkv.at[(ALL,) + piece], b.w.at[(j, pl.ds(0, 3)) + piece], w_one + m + n, at_col(g + off))
+            push(inputs.wo.at[piece], b.w.at[(j, 3) + piece], w_one + 6 + m + n, at_col(g + off))
 
     left_rows, right_rows = pl.ds(0, GRID_DEV), pl.ds(2 * GRID_DEV, GRID_DEV)
     grid_sem = take(2)
@@ -349,17 +368,11 @@
 
     lax.fori_loop(0, 8, build, 0)
 
-    others = pl.ds(1, 3)
     for n in range(3):
-        arrived(b.w.at[(n + 1, ALL) + piece_a], z_sem + n)
-        arrived(b.w.at[(n + 1, ALL) + piece_b], z_sem + 3 + n)
-    first_a, first_b = take(3), take(3)
-    for d in range(1, 4):
-        part_a = b.w.at[(others, ALL) + piece_a]
-        part_b = b.w.at[(others, ALL) + piece_b]
-        push(part_a, part_a, first_a + d - 1, at_x(d))
-        push(part_b, part_b, first_b + d - 1, at_y(d))
-
+        for m, piece in ((0, piece_a), (3, piece_b)):
+            arrived(b.w.at[(n + 1, pl.ds(0, 3)) + piece], w_one + m + n)
+            arrived(b.w.at[(n + 1, 3) + piece], w_one + 6 + m + n)
+    across(ALL, w_two, piece_a, piece_b, at_x, at_y)
     own_grid.wait()
     arrived(b.ext.at[left_rows], grid_sem)
     arrived(b.ext.at[right_rows], grid_sem + 1)
@@ -373,25 +386,10 @@
     for t in range(4):
         push(mine, b.nodes.at[lax.rem(r + 6, 8)], next_sem + r, at_col(near + t))
 
-    for d in range(1, 4):
-        arrived(b.w.at[(others, ALL) + piece_a], first_a + d - 1)
-        arrived(b.w.at[(others, ALL) + piece_b], first_b + d - 1)
-    row_a = (tile16(y), LOW)
-    row_b = (tile16(x), HIGH)
-    QKV, OUT = pl.ds(0, 3), pl.ds(3, 1)
-    second = {}
-    for kinds, name in ((QKV, "qkv"), (OUT, "out")):
-        second[name] = take(6)
-        for d in range(1, 4):
-            part_a = b.w.at[(others, kinds) + row_a]
-            part_b = b.w.at[(others, kinds) + row_b]
-            push(part_a, part_a, second[name] + d - 1, at_y(d))
-            push(part_b, part_b, second[name] + 2 + d, at_x(d))
-
-    def wait_second(kinds, name):
-        for d in range(1, 4):
-            arrived(b.w.at[(others, kinds) + row_a], second[name] + d - 1)
-            arrived(b.w.at[(others, kinds) + row_b], second[name] + 2 + d)
+    across_arrived(ALL, w_two, piece_a, piece_b)
+    w_kv, w_query, w_out = take(6), take(6), take(6)
+    for kinds, sems in ((KV, w_kv), (QUERY, w_query), (OUT, w_out)):
+        across(kinds, sems, row_a, row_b, at_y, at_x)
 
     own_cot.wait()
     cot_sem = take(3)
@@ -413,14 +411,15 @@
         b.normed[tile128(k), :] = (centred * lax.rsqrt(spread + 1e-05)).astype(BF16)
         return carry
 
-    lax.fori_loop(0, 8, normalise, 0)
+    lax.fori_loop(0, 8, normalise, 0, unroll=2)
 
     arrived(b.cot.at[across], cot_sem)
     push(b.cot.at[across], b.cot.at[across], cot_sem + 2, at_col(g - r + sibling))
-    wait_second(QKV, "qkv")
+    own_qkv.wait()
+    own_wo.wait()
+    across_arrived(KV, w_kv, row_a, row_b)
 
     sems_1 = [take(6) for _ in range(4)]
-    sems_2 = [take(6) for _ in range(4)]
     part_sem = take(3)
 
     def plane_first(c):
@@ -429,90 +428,98 @@
             push(b.grads.at[c, :, tile16(to_y), LOW], b.in_a1.at[c, d - 1], sems_1[c] + d - 1, at_y(d))
             push(b.grads.at[c, :, tile16(to_x), HIGH], b.in_b1.at[c, d - 1], sems_1[c] + 2 + d, at_x(d))
 
-    def plane_second(c):
-        for d in range(1, 4):
-            arrived(b.in_a1.at[c, d - 1], sems_1[c] + d - 1)
-            arrived(b.in_b1.at[c, d - 1], sems_1[c] + 2 + d)
-        sum_a = b.grads[c, :, tile16(y), LOW].astype(F32)
-        sum_b = b.grads[c, :, tile16(x), HIGH].astype(F32)
-        for d in range(3):
-            sum_a += b.in_a1[c, d].astype(F32)
-            sum_b += b.in_b1[c, d].astype(F32)
-        b.sum_a1[c] = sum_a.astype(BF16)
-        b.sum_b1[c] = sum_b.astype(BF16)
-        for d in range(1, 4):
-            to_y, to_x = lax.rem(y + d, 4), lax.rem(x + d, 4)
-            push(b.sum_a1.at[c, :, :, tile128(to_x)], b.in_a2.at[c, d - 1], sems_2[c] + d - 1, at_x(d))
-            push(b.sum_b1.at[c, :, :, tile128(to_y)], b.in_b2.at[c, d - 1], sems_2[c] + 2 + d, at_y(d))
-
-    def plane_last(c):
-        for d in range(1, 4):
-            arrived(b.in_a2.at[c, d - 1], sems_2[c] + d - 1)
-            arrived(b.in_b2.at[c, d - 1], sems_2[c] + 2 + d)
-        sum_a = b.sum_a1[c, :, :, tile128(x)].astype(F32)
-        sum_b = b.sum_b1[c, :, :, tile128(y)].astype(F32)
-        for d in range(3):
-            sum_a += b.in_a2[c, d].astype(F32)
-            sum_b += b.in_b2[c, d].astype(F32)
-        b.plane[:, c, 0] = sum_a.astype(BF16)
-        b.plane[:, c, 1] = sum_b.astype(BF16)
-
-    class Column:
+    class Unit:
         def __init__(self, first):
+            self.kinds = (first, first + 1)
             self.c = pl.ds(first, 2)
-            self.near, self.far, self.one, self.two = take(4), take(), take(6), take(6)
-
-        def to_owners(self):
+            self.two, self.column, self.back, self.rest = take(6), take(7), take(6), take(6)
+
+        def second(self):
+            for c in self.kinds:
+                for d in range(1, 4):
+                    arrived(b.in_a1.at[c, d - 1], sems_1[c] + d - 1)
+                    arrived(b.in_b1.at[c, d - 1], sems_1[c] + 2 + d)
+                sum_a = b.grads[c, :, tile16(y), LOW].astype(F32)
+                sum_b = b.grads[c, :, tile16(x), HIGH].astype(F32)
+                for d in range(3):
+                    sum_a += b.in_a1[c, d].astype(F32)
+                    sum_b += b.in_b1[c, d].astype(F32)
+                b.sum_a1[c] = sum_a.astype(BF16)
+                b.sum_b1[c] = sum_b.astype(BF16)
             c = self.c
-            push(b.plane.at[1, c], b.in_z.at[0, c], self.near, at_col(g - 4))
-            push(b.plane.at[2, c], b.in_z.at[1, c], self.near + 1, at_col(g + 4))
-            push(b.plane.at[3, c, 0], b.in_z4.at[0, c], self.near + 2, at_col(g + 8))
-            push(b.plane.at[3, c, 1], b.in_z4.at[1, c], self.near + 3, at_col(g - 8))
-
-        def to_far(self):
+            for d in range(1, 4):
+                to_y, to_x = lax.rem(y + d, 4), lax.rem(x + d, 4)
+                push(b.sum_a1.at[c, :, :, tile128(to_x)], b.in_a2.at[d - 1, c], self.two + d - 1, at_x(d))
+                push(b.sum_b1.at[c, :, :, tile128(to_y)], b.in_b2.at[d - 1, c], self.two + 2 + d, at_y(d))
+
+        def plane_sum(self):
+            for d in range(3):
+                arrived(b.in_a2.at[d, self.c], self.two + d)
+                arrived(b.in_b2.at[d, self.c], self.two + 3 + d)
+            for c in self.kinds:
+                sum_a = b.sum_a1[c, :, :, tile128(x)].astype(F32)
+                sum_b = b.sum_b1[c, :, :, tile128(y)].astype(F32)
+                for d in range(3):
+                    sum_a += b.in_a2[d, c].astype(F32)
+                    sum_b += b.in_b2[d, c].astype(F32)
+                b.plane[:, c, 0] = sum_a.astype(BF16)
+                b.plane[:, c, 1] = sum_b.astype(BF16)
+
+        def to_all(self):
+            self.plane_sum()
+            for d in (4, 3, 5, 2, 6, 1, 7):
+                push(b.plane.at[SHARD_AT[d], self.c], b.in_z.at[d, self.c], self.column + d - 1, at_col(g + 4 * d))
+
+        def all_sum(self):
             c = self.c
-            for n in range(2):
-                arrived(b.in_z.at[n, c], self.near + n)
-                arrived(b.in_z4.at[n, c], self.near + 2 + n)
-            for n in range(2):
-                total = b.plane[0, c, n].astype(F32) + b.in_z4[n, c].astype(F32)
-                total += b.in_z[0, c, n].astype(F32) + b.in_z[1, c, n].astype(F32)
-                b.half_sum[c, n] = total.astype(BF16)
-            push(b.half_sum.at[c], b.far.at[c], self.far, at_col(g + 16))
-
-        def to_plane(self):
+            for d in range(1, 8):
+                arrived(b.in_z.at[d, c], self.column + d - 1)
+            pairs = [b.plane[0, c].astype(F32) + b.in_z[4, c].astype(F32)]
+            pairs += [b.in_z[d, c].astype(F32) + b.in_z[d + 4, c].astype(F32) for d in (1, 2, 3)]
+            self.to_plane(((pairs[0] + pairs[2]) + (pairs[1] + pairs[3])).astype(BF16))
+
+        def to_plane(self, total):
             c = self.c
-            arrived(b.far.at[c], self.far)
-            total = (b.half_sum[c].astype(F32) + b.far[c].astype(F32)).astype(BF16)
-            b.gathered[c, piece_a[0], piece_a[1]] = total[:, 0]
-            b.gathered[c, piece_b[0], piece_b[1]] = total[:, 1]
+            b.gathered[(c,) + piece_a] = total[:, 0]
+            b.gathered[(c,) + piece_b] = total[:, 1]
             for d in range(1, 4):
                 part_a, part_b = b.gathered.at[(c,) + piece_a], b.gathered.at[(c,) + piece_b]
-                push(part_a, part_a, self.one + d - 1, at_x(d))
-                push(part_b, part_b, self.one + 2 + d, at_y(d))
+                push(part_a, part_a, self.back + d - 1, at_x(d))
+                push(part_b, part_b, self.back + 2 + d, at_y(d))
 
         def to_rest(self):
             c = self.c
-            for d in range(1, 4):
-                arrived(b.gathered.at[(c,) + piece_a], self.one + d - 1)
-                arrived(b.gathered.at[(c,) + piece_b], self.one + 2 + d)
+            for d in range(3):
+                arrived(b.gathered.at[(c,) + piece_a], self.back + d)
+                arrived(b.gathered.at[(c,) + piece_b], self.back + 3 + d)
             for d in range(1, 4):
                 part_a, part_b = b.gathered.at[(c,) + row_a], b.gathered.at[(c,) + row_b]
-                push(part_a, part_a, self.two + d - 1, at_y(d))
-                push(part_b, part_b, self.two + 2 + d, at_x(d))
+                push(part_a, part_a, self.rest + d - 1, at_y(d))
+                push(part_b, part_b, self.rest + 2 + d, at_x(d))
 
         def finish(self):
             c = self.c
-            for d in range(1, 4):
-                arrived(b.gathered.at[(c,) + row_a], self.two + d - 1)
-                arrived(b.gathered.at[(c,) + row_b], self.two + 2 + d)
-            return here(b.gathered.at[c], weight_grads.at[c])
-
-    early, late = Column(2), Column(0)
+            for d in range(3):
+                arrived(b.gathered.at[(c,) + row_a], self.rest + d)
+                arrived(b.gathered.at[(c,) + row_b], self.rest + 3 + d)
+            results.append(here(b.gathered.at[c], weight_grads.at[c]))
+
+    results = []
+
+    def finish(c):
+        for d in range(1, 4):
+            arrived(b.gathered.at[(c,) + row_a], sems_4[c] + d - 1)
+            arrived(b.gathered.at[(c,) + row_b], sems_4[c] + 2 + d)
+        results.append(here(b.gathered.at[c], weight_grads.at[c]))
+
+    early, late = Unit(2), Unit(0)
 
     class Hooks:
+        def before_query(self):
+            across_arrived(QUERY, w_query, row_a, row_b)
+
         def before_out(self):
-            wait_second(OUT, "out")
+            across_arrived(OUT, w_out, row_a, row_b)
             arrived(b.cot.at[sibling], cot_sem + 1)
             arrived(b.cot.at[lax.rem(sibling + 2, 4)], cot_sem + 2)
 
@@ -523,34 +530,24 @@
         def have_grad(self, c):
             plane_first(c)
 
-        def after_backward(self):
-            plane_second(3)
-            plane_second(2)
-
     attention(grp, b.normed, b.w, b.cot, b.grads, b.part, s, Hooks())
 
-    plane_last(3)
-    plane_last(2)
-    early.to_owners()
+    early.second()
+    early.to_all()
+    late.second()
     out = dot(b.nodes[r + 2], b.enc[...]) + b.part[r].astype(F32)
     for d in range(3):
         arrived(b.part_in.at[d], part_sem + d)
         out += b.part_in[d].astype(F32)
     b.out[...] = out.astype(BF16)
-    results = [here(b.out, layer_out)]
-    plane_second(0)
-    plane_second(1)
-    early.to_far()
-    plane_last(0)
-    plane_last(1)
-    late.to_owners()
-    early.to_plane()
-    late.to_far()
+    results.append(here(b.out, layer_out))
+    late.to_all()
+    early.all_sum()
     early.to_rest()
-    late.to_plane()
-    results.append(early.finish())
+    late.all_sum()
+    early.finish()
     late.to_rest()
-    results.append(late.finish())
+    late.finish()
     for copy in results:
         copy.wait()
     for copy in started:

time: 93.3 us -> 86.3 us (0.925)
  Pallas kernels: 92.5 us -> 85.3 us
    pallas_call x1, Pallas kernels: 90.2 us -> 83 us  [on_device(): pl.pallas_call(step_kernel, out_shape=(jax.ShapeDtypeStruct((128, 1024),...]
where the time goes in v3:
time: 86.3 us; the launch traced here: 85.9 us
  Pallas kernels  85.3 us (99%)
    pallas_call x1, Pallas kernels, on_device(): pl.pallas_call(step_kernel, out_shape=(jax.ShapeDtypeStruct((128, 1024),...  83 us
    pallas_call x1, Pallas kernels, on_device(): pl.pallas_call(finish_kernel, out_shape=(jax.ShapeDtypeStruct((128, 1024)...  2.24 us

profile of v3, /device:TPU:6, one launch (start us, length us, event | category | flops | bytes accessed | tf_op | source)
XLA Modules:
  0.0 85.9 jit_solution(1289322407445917786)
XLA Ops:
  0.6 83.0 %shard_map.103 = (bf16[128,1024]{1,0:T(8,128)(2,1)}, bf16[4,64,1024]{2,1,0:T(8,128)(2,1)}) custom-call(bf16[1728,128]{1,0:T(8,128)(2,1)} %bitcast.6, s32[32,128]{1,0:T(8,128)} %bitcast.8, s32[1,128]{1,0:T(1,128)} %bitcast.10, f32[32,128]{1,0:T(8,128)} %bitcast.9, bf16[128,1024]{1,0:T(8,128)(2,1)} %refs_4_.1, bf16[3,64,1024]{2,1,0:T(8,128)(2,1)} %refs_5_.1, ...), custom_call_target="tpu_custom_call" | custom-call | tf_op jit(solution)/shard_map/pallas_call | solution.py:568
  83.7 2.2 %shard_map.104 = (bf16[128,1024]{1,0:T(8,128)(2,1)}, f32[3,64,1024]{2,1,0:T(8,128)}, f32[64,1024]{1,0:T(8,128)}) custom-call(bf16[128,1024]{1,0:T(8,128)(2,1)} %get-tuple-element.8.layer_in, bf16[4,64,1024]{2,1,0:T(8,128)(2,1)} %get-tuple-element.9.grads), custom_call_target="tpu_custom_call" | custom-call | tf_op jit(solution)/shard_map/pallas_call | solution.py:596

commit v4 on v3

--- a/solution.py
+++ b/solution.py
@@ -555,16 +555,25 @@
     assert used[0] <= SEMS and len(started) <= SEMS and local[0] <= 16
 
 
-def finish_kernel(layer_in, grads, layer_out, grad_qkv, grad_out):
-    layer_out[...] = layer_in[...]
-    grad_qkv[...] = grads[0:3].astype(F32)
-    grad_out[...] = grads[3].astype(F32)
+def finish_kernel(layer_in, grads, layer_out, grad_qkv, grad_out, narrow, wide, in_sem, out_sem):
+    layer = pltpu.make_async_copy(layer_in, layer_out, in_sem.at[4])
+    reads = [pltpu.make_async_copy(grads.at[c], narrow.at[c], in_sem.at[c]) for c in range(4)]
+    for copy in (*reads, layer):
+        copy.start()
+    writes = []
+    for c in range(4):
+        reads[c].wait()
+        wide[c] = narrow[c].astype(F32)
+        writes.append(pltpu.make_async_copy(wide.at[c], grad_qkv.at[c] if c < 3 else grad_out, out_sem.at[c]))
+        writes[c].start()
+    for copy in (*writes, layer):
+        copy.wait()
 
 
 def on_device(
     grid_fields, edge_grid, edge_count, edge_weight, enc_weight, qkv_weight, out_weight, cotangent
 ):
-    vmem, anywhere = pl.BlockSpec(memory_space=pltpu.VMEM), pl.BlockSpec(memory_space=pl.ANY)
+    anywhere = pl.BlockSpec(memory_space=pl.ANY)
     layer_out, grads = pl.pallas_call(
         step_kernel,
         out_shape=(
@@ -600,8 +609,14 @@
             jax.ShapeDtypeStruct((3, 64, 1024), F32),
             jax.ShapeDtypeStruct((64, 1024), F32),
         ),
-        in_specs=[vmem, vmem],
-        out_specs=(vmem, vmem, vmem),
+        in_specs=[anywhere] * 2,
+        out_specs=(anywhere,) * 3,
+        scratch_shapes=[
+            pltpu.VMEM((4, 64, 1024), BF16),
+            pltpu.VMEM((4, 64, 1024), F32),
+            pltpu.SemaphoreType.DMA((5,)),
+            pltpu.SemaphoreType.DMA((4,)),
+        ],
     )(layer_out, grads)
     return layer_out[None], grad_qkv, grad_out
 

time: 86.3 us -> 93.4 us (1.082)
  Pallas kernels: 85.3 us -> 92.1 us
    pallas_call x1, Pallas kernels: 2.24 us -> 9.13 us  [on_device(): pl.pallas_call(finish_kernel, out_shape=(jax.ShapeDtypeStruct((128, 1024)...]
where the time goes in v4:
time: 93.4 us; the launch traced here: 92.9 us
  Pallas kernels  92.1 us (99%)
    pallas_call x1, Pallas kernels, on_device(): pl.pallas_call(step_kernel, out_shape=(jax.ShapeDtypeStruct((128, 1024),...  83 us
    pallas_call x1, Pallas kernels, on_device(): pl.pallas_call(finish_kernel, out_shape=(jax.ShapeDtypeStruct((128, 1024)...  9.13 us

profile of v4, /device:TPU:6, one launch (start us, length us, event | category | flops | bytes accessed | tf_op | source)
XLA Modules:
  0.0 92.9 jit_solution(8031177415869732269)
XLA Ops:
  0.6 83.0 %shard_map.103 = (bf16[128,1024]{1,0:T(8,128)(2,1)}, bf16[4,64,1024]{2,1,0:T(8,128)(2,1)}) custom-call(bf16[1728,128]{1,0:T(8,128)(2,1)} %bitcast.6, s32[32,128]{1,0:T(8,128)} %bitcast.8, s32[1,128]{1,0:T(1,128)} %bitcast.10, f32[32,128]{1,0:T(8,128)} %bitcast.9, bf16[128,1024]{1,0:T(8,128)(2,1)} %refs_4_.1, bf16[3,64,1024]{2,1,0:T(8,128)(2,1)} %refs_5_.1, ...), custom_call_target="tpu_custom_call" | custom-call | tf_op jit(solution)/shard_map/pallas_call | solution.py:577
  83.7 9.1 %shard_map.104 = (bf16[128,1024]{1,0:T(8,128)(2,1)}, f32[3,64,1024]{2,1,0:T(8,128)}, f32[64,1024]{1,0:T(8,128)}) custom-call(bf16[128,1024]{1,0:T(8,128)(2,1)} %get-tuple-element.8.layer_in, bf16[4,64,1024]{2,1,0:T(8,128)(2,1)} %get-tuple-element.9.grads), custom_call_target="tpu_custom_call" | custom-call | tf_op jit(solution)/shard_map/pallas_call | solution.py:605
